TPU v7x, 512 devices: a whole 4x8x8 slice. The times are simulated.
512 devices in a mesh: gx: 8 (over y), gy: 4 (over z_lo), gz: 16 (over z_hi, x, core).
Axes of the slice: x: 4, y: 8, z: 8 (z_hi: 2, z_lo: 4; z = z_hi * 4 + z_lo), core: 2. Of those that a mesh axis runs over, the one named last changes fastest.
Arguments:
- field: float32 [1024, 8, 32, 512], P('gx', None, 'gz', 'gy'), may hold values from -72 to 72
- factor_one: float32 [1024, 256], P('gx'), may hold values from -0.25 to 0.25
- factor_two: float32 [512, 128], P('gy'), may hold values from -0.375 to 0.375
Outputs:
- gram_one: float32 [1024, 1024], P('gx', ('gy', 'gz'))
- gram_two: float32 [512, 512], P('gy')
- core: float32 [256, 8, 32, 128], P('gx', None, 'gz', 'gy')
All inputs are finite; a program needn't handle non-finite values.
Results may differ from a plain program's by a relative error of at most 0.000078.
Values sent between devices are 32-bit elements; how exact they have to be, the bound alone decides.
No kernel may reach another device: no remote copies, remote signals or barrier semaphores. Data moves between devices by JAX's collectives and lax.ppermute only.
A program may use at most 64 MiB of HBM per device.

v0:
```python
import jax
import jax.numpy as jnp
from jax import lax
from jax.sharding import PartitionSpec as P

R1 = 256


def per_device(field, factor_one, factor_two):
    highest = lax.Precision.HIGHEST
    rows_here, levels, cells_three, cols_here = field.shape
    field_rows = field.reshape(rows_here, -1)
    fibre_count = lax.axis_size("gx")
    rank_share = R1 // fibre_count
    third_total = cells_three * lax.axis_size("gz")
    piece = lax.all_gather(field, "gx", axis=0, tiled=True)
    piece_rows = piece.reshape(piece.shape[0], -1)
    block = lax.dot_general(field_rows, piece_rows, (((1,), (1,)), ((), ())), precision=highest)
    reduced = lax.psum_scatter(
        lax.dot_general(factor_one, field_rows, (((0,), (0,)), ((), ())), precision=highest),
        "gx",
        scatter_dimension=0,
        tiled=True,
    )
    gram_one = lax.psum_scatter(block, ("gy", "gz"), scatter_dimension=1, tiled=True) / (
        cols_here * lax.axis_size("gy") * third_total * levels
    )
    projected = reduced.reshape(rank_share, levels, cells_three, cols_here)
    gathered = lax.all_gather(projected, "gy", axis=3, tiled=True)
    gram_terms = lax.dot_general(
        projected, gathered, (((0, 1, 2), (0, 1, 2)), ((), ())), precision=highest
    )
    gram_two = lax.psum(gram_terms, ("gx", "gz")) / (R1 * third_total * levels)
    core_rows = lax.psum_scatter(
        lax.dot_general(factor_two, projected, (((0,), (3,)), ((), ())), precision=highest),
        "gy",
        scatter_dimension=0,
        tiled=True,
    )
    core = jnp.transpose(core_rows, (1, 2, 3, 0))
    return (gram_one, gram_two, core)


def solution(mesh):
    return jax.shard_map(
        per_device,
        mesh=mesh,
        in_specs=(P("gx", None, "gz", "gy"), P("gx", None), P("gy", None)),
        out_specs=(P("gx", ("gy", "gz")), P("gy", None), P("gx", None, "gz", "gy")),
        check_vma=False,
    )
```

profile of v0, /device:TPU:1, one launch (start us, length us, event | category | flops | bytes accessed | tf_op | source)
XLA Modules:
  0.0 1993.6 jit_solution(3306037392652732695)
XLA Ops:
  7.2 0.0 copy-start
  7.2 0.0 copy-start.1
  7.2 0.0 copy-start.2
  7.2 0.0 reduce-scatter.8.cloned.1.call-start
  7.2 2.2 reshape.13
  9.4 0.0 copy-done
  9.4 3.2 fusion.4
  12.6 0.0 reduce-scatter.8.cloned.1.call-update
  12.6 0.0 all-gather.5.cloned.1.call-start
  12.7 46.1 %reduce-scatter.8.cloned.1.call-done = f32[32,2048]{1,0:T(8,128)} async-done(((f32[256,2048]{1,0:T(8,128)}), f32[32,2048]{1,0:T(8,128)}) %reduce-scatter.8.cloned.1.call-update) | async-done | bytes 262160 | tf_op jit(solution)/shard_map/reduce_scatter | solution.py:19
  58.8 1.2 reshape.14
  60.0 0.8 copy.15
  60.7 0.0 all-gather.5.cloned.1.call-update
  60.8 0.0 all-gather.3.cloned.1.call-start
  60.8 0.0 copy-done.1
  60.8 1.4 copy.13
  62.2 0.0 all-gather.3.cloned.1.call-update
  62.2 0.0 reduce-scatter.10.cloned.1.call-start
  62.3 0.0 copy-done.2
  62.3 0.4 convolution_bitcast_fusion.1
  62.6 4.4 copy.21
  67.1 8.6 reshape.18
  75.6 0.0 reduce-scatter.10.cloned.1.call-update
  75.6 0.0 all-reduce.2.cloned.1.call-start
  75.7 28.5 %all-gather.5.cloned.1.call-done = f32[32,8,2,512]{3,0,2,1:T(8,128)} async-done(((f32[32,8,2,128]{3,0,2,1:T(8,128)}), f32[32,8,2,512]{3,0,2,1:T(8,128)}) %all-gather.5.cloned.1.call-update) | async-done | bytes 1048592 | tf_op jit(solution)/shard_map/all_gather | solution.py:29
  104.2 2.8 convolution_bitcast_fusion.2
  107.0 0.0 all-reduce.2.cloned.1.call-update
  107.0 0.2 reduce-scatter.6.cloned.1.call-start
  107.2 93.2 %all-gather.3.cloned.1.call-done = f32[1024,8,2,128]{3,0,2,1:T(8,128)} async-done(((f32[128,8,2,128]{3,0,2,1:T(8,128)}), f32[1024,8,2,128]{3,0,2,1:T(8,128)}) %all-gather.3.cloned.1.call-update) | async-done | bytes 8388624 | tf_op jit(solution)/shard_map/all_gather | solution.py:16
  200.5 9.8 convolution_bitcast_fusion
  210.3 0.0 reduce-scatter.6.cloned.1.call-update
  210.3 18.3 reduce-scatter.10.cloned.1.call-done
  228.6 2.4 reshape.19
  231.0 0.6 copy.22
  231.7 0.8 copy.17
  232.5 1427.1 %all-reduce.2.cloned.1.call-done = f32[128,512]{1,0:T(8,128)} async-done(((f32[128,512]{1,0:T(8,128)}), f32[128,512]{1,0:T(8,128)}) %all-reduce.2.cloned.1.call-update) | async-done | bytes 262160 | tf_op jit(solution)/shard_map/psum | solution.py:33
  1659.7 1.7 broadcast_multiply_fusion
  1661.3 324.1 %reduce-scatter.6.cloned.1.call-done = f32[128,16]{0,1:T(8,128)} async-done(((f32[128,1024]{0,1:T(8,128)}), f32[128,16]{0,1:T(8,128)}) %reduce-scatter.6.cloned.1.call-update) | async-done | bytes 8208 | tf_op jit(solution)/shard_map/reduce_scatter | solution.py:25
  1985.4 1.3 broadcast_multiply_fusion.1
Async XLA Ops:
  7.2 2.2 copy-start
  7.2 53.6 %copy-start.1 = (f32[128,8,2,128]{3,2,1,0:T(2,128)S(1)}, f32[128,8,2,128]{3,2,1,0:T(2,128)}, u32[]{:S(2)}) copy-start(f32[128,8,2,128]{3,2,1,0:T(2,128)} %param.3) | copy-start | bytes 3145732
  7.2 55.1 %copy-start.2 = (f32[128,128]{1,0:T(8,128)S(1)}, f32[128,128]{1,0:T(8,128)}, u32[]{:S(2)}) copy-start(f32[128,128]{1,0:T(8,128)} %param.5) | copy-start | bytes 196612
  7.2 51.6 %reduce-scatter.8.cloned.1.call-start = ((), (), s32[]{:S(2)}) async-start(), calls=%async_computation.5 | async-start | bytes 2359296 | tf_op jit(solution)/shard_map/reduce_scatter | solution.py:19
  12.6 91.6 %all-gather.5.cloned.1.call-start = ((), (), s32[]{:S(2)}) async-start(), calls=%async_computation.6 | async-start | bytes 1310720 | tf_op jit(solution)/shard_map/all_gather | solution.py:29
  60.8 139.7 %all-gather.3.cloned.1.call-start = ((), (), s32[]{:S(2)}) async-start(), calls=%async_computation.3 | async-start | bytes 9437184 | tf_op jit(solution)/shard_map/all_gather | solution.py:16
  62.2 166.4 %reduce-scatter.10.cloned.1.call-start = ((), (), s32[]{:S(2)}) async-start(), calls=%async_computation.8 | async-start | bytes 327680
  75.6 1584.0 %all-reduce.2.cloned.1.call-start = ((), (), s32[]{:S(2)}) async-start(), calls=%async_computation.7 | async-start | bytes 524288 | tf_op jit(solution)/shard_map/psum | solution.py:33
  107.0 1878.4 %reduce-scatter.6.cloned.1.call-start = ((), (), s32[]{:S(2)}) async-start(), calls=%async_computation.4 | async-start | bytes 532480 | tf_op jit(solution)/shard_map/reduce_scatter | solution.py:25
Sparse Core Ops, SparseCore 0:
  12.8 45.9 reduce-scatter.7
  61.4 42.7 all-gather.4
  106.3 94.1 all-gather.2
  203.1 25.4 reduce-scatter.9
  232.2 1427.4 all-reduce.1
  1662.3 323.0 reduce-scatter.5
where the time goes:
time: 2010 us; the launch traced here: 1990 us
  waiting for transfers between devices  1940 us (97%)
  local copies, waits for them, and re-layouts  22.4 us (1%)
    psum x1, waiting for transfers between devices, per_device(): gram_two = lax.psum(gram_terms, ('gx', 'gz')) / (R1 * third_total * levels)  1430 us
    reduce_scatter x1, waiting for transfers between devices, per_device(): lax.psum_scatter(block, ('gy', 'gz'), scatter_dimension=1, tiled=True)  324 us
    all_gather x1, waiting for transfers between devices, per_device(): piece = lax.all_gather(field, 'gx', axis=0, tiled=True)  93.2 us
    reduce_scatter x1, waiting for transfers between devices, per_device(): lax.psum_scatter(lax.dot_general(factor_one, field_rows, (((0,), (0,)), (...  46.1 us
  transfers between devices with their start and end apart: 6, of which 6 were waited for; matrix products, arithmetic and copies ran while one was open for 2% of the time, Pallas kernels for 0%

commit v1 on v0

v1 whole, which is shorter than its diff:
```python
import jax
import jax.numpy as jnp
from jax import lax
from jax.sharding import Mesh
from jax.sharding import PartitionSpec as P

NY, NZL, NZH, NX, NC = 8, 4, 2, 4, 2
PREC = lax.Precision.HIGH


def exchange(a, axes):
    return lax.all_to_all(a, axes, 0, 0)


def per_device(field, u, v):
    f32 = jnp.float32
    core_id = lax.axis_index("c")

    f = jnp.transpose(field, (1, 2, 0, 3))
    f = exchange(f, "y")
    u_all = lax.all_gather(u, "y", axis=0)

    z = lax.dot_general(
        jnp.transpose(f, (1, 0, 2, 3)).reshape(2, 1024, 128),
        u_all.reshape(1024, 256),
        (((1,), (0,)), ((), ())),
        precision=PREC,
        preferred_element_type=f32,
    )
    z = jnp.transpose(z, (0, 2, 1)).reshape(512, 128)

    vt = jnp.transpose(v).reshape(NZL, 32, 128)
    zv = jnp.concatenate([jnp.broadcast_to(z, (NZL, 512, 128)), vt], axis=1)
    zv = exchange(zv, "zl")
    zg, vg = zv[:, :512], zv[:, 512:]

    g2 = lax.dot_general(
        z, jnp.transpose(zg, (1, 0, 2)).reshape(512, 512), (((0,), (0,)), ((), ())),
        precision=PREC, preferred_element_type=f32,
    )

    zr = zg.reshape(NZL, 2, 8, 4, 8, 128)
    zr = jnp.transpose(zr, (2, 1, 4, 3, 0, 5)).reshape(128, 4 * 512)
    vd = jnp.eye(4, dtype=f32)[:, None, :, None, None] * jnp.transpose(vg, (1, 0, 2))[None, :, None]
    vd = vd.reshape(128, 4 * 512)
    core_rows = lax.dot_general(
        zr, vd, (((1,), (1,)), ((), ())), precision=PREC, preferred_element_type=f32
    )

    other = lax.ppermute(f, "c", [(0, 1), (1, 0)])

    def rows_of(a):
        return jnp.transpose(a, (0, 2, 1, 3)).reshape(1024, 256)

    cells = jnp.concatenate([rows_of(f), rows_of(other)], axis=1)
    mine = cells.reshape(8, 4, 2, 16, 512)
    mine = lax.dynamic_index_in_dim(mine, core_id, 2, keepdims=False)
    mine = jnp.transpose(mine, (1, 0, 2, 3)).reshape(512, 512)
    g1 = lax.dot_general(
        mine, cells, (((1,), (1,)), ((), ())), precision=PREC, preferred_element_type=f32
    ).reshape(NX, 128, 1024)
    g1 = jnp.sum(exchange(g1, "x"), axis=0)
    g1 = jnp.transpose(g1.reshape(128, 8, 128), (1, 0, 2))

    g2 = jnp.sum(exchange(g2.reshape(8, 16, 512), ("x", "c")), axis=0)
    g2 = jnp.transpose(g2.reshape(16, 4, 128), (1, 0, 2)).reshape(64, 128)

    send = jnp.concatenate(
        [g1, core_rows.reshape(8, 16, 128), jnp.broadcast_to(g2, (8, 64, 128))], axis=1
    )
    got = exchange(send, "y")
    g1 = jnp.sum(got[:, :128], axis=0)
    core = got[:, 128:144].reshape(8, 2, 8, 4, 32)
    core = jnp.transpose(core, (3, 2, 0, 1, 4)).reshape(32, 8, 2, 32)
    g2 = jnp.sum(got[:, 144:], axis=0)
    g2 = g2 + lax.ppermute(g2, "zh", [(0, 1), (1, 0)])
    g2 = exchange(jnp.broadcast_to(g2, (8, 64, 128)), ("x", "c"))
    g2 = jnp.transpose(g2.reshape(8, 4, 16, 128), (0, 2, 1, 3)).reshape(128, 512)
    gram_two = g2 / 65536.0

    g1 = jnp.sum(exchange(g1.reshape(8, 16, 128), ("zl", "zh")), axis=0)
    gram_one = jnp.transpose(g1) / 131072.0
    return gram_one, gram_two, core


def solution(mesh):
    split = Mesh(mesh.devices.reshape(NY, NZL, NZH, NX, NC), ("y", "zl", "zh", "x", "c"))
    gz = ("zh", "x", "c")
    return jax.shard_map(
        per_device,
        mesh=split,
        in_specs=(P("y", None, gz, "zl"), P("y", None), P("zl", None)),
        out_specs=(P("y", ("zl",) + gz), P("zl", None), P("y", None, gz, "zl")),
        check_vma=False,
    )
```

time: 2010 us -> 217 us (0.11)
  waiting for transfers between devices: 1940 us -> 80.4 us
  starting transfers between devices: 0.43 us -> 52.7 us
  blocking collectives: 0 us -> 25.3 us
    psum x1 -> x0, waiting for transfers between devices: 1430 us -> none  [per_device(): gram_two = lax.psum(gram_terms, ('gx', 'gz')) / (R1 * third_total * levels)]
    reduce_scatter x2 -> x0, waiting for transfers between devices: 370 us -> none  [the longest x1 324 us: per_device(): lax.psum_scatter(block, ('gy', 'gz'), scatter_dimension=1, tiled=True)]
    all_gather x2 -> x1, waiting for transfers between devices: 122 us -> 19.7 us  [per_device(): u_all = lax.all_gather(u, 'y', axis=0)]
    all_to_all x0 -> x6, waiting for transfers between devices: none -> 58 us  [exchange(): return lax.all_to_all(a, axes, 0, 0)]
    all_to_all x0 -> x6, starting transfers between devices: none -> 38.6 us  [exchange(): return lax.all_to_all(a, axes, 0, 0)]
    all_to_all x0 -> x1, blocking collectives: none -> 25.3 us  [exchange(): return lax.all_to_all(a, axes, 0, 0)]
  transfers between devices with their start and end apart: 6 -> 9, of which waited for: 6 -> 7; matrix products, arithmetic and copies ran while one was open for 2% -> 12% of each run, Pallas kernels for 0% -> 0%
where the time goes in v1:
time: 217 us; the launch traced here: 216 us
  waiting for transfers between devices  80.4 us (37%)
  starting transfers between devices  52.7 us (24%)
  blocking collectives  25.3 us (12%)
  local copies, waits for them, and re-layouts  24.7 us (11%)
  between operations  14.3 us (7%)
  matrix products  12.9 us (6%)
  other arithmetic  5.38 us (2%)
    all_to_all x6, waiting for transfers between devices, exchange(): return lax.all_to_all(a, axes, 0, 0)  58 us
    all_to_all x6, starting transfers between devices, exchange(): return lax.all_to_all(a, axes, 0, 0)  38.6 us
    all_to_all x1, blocking collectives, exchange(): return lax.all_to_all(a, axes, 0, 0)  25.3 us
    all_gather x1, waiting for transfers between devices, per_device(): u_all = lax.all_gather(u, 'y', axis=0)  19.7 us
    ppermute x1, starting transfers between devices, per_device(): g2 = g2 + lax.ppermute(g2, 'zh', [(0, 1), (1, 0)])  7.28 us
    ppermute x1, starting transfers between devices, per_device(): other = lax.ppermute(f, 'c', [(0, 1), (1, 0)])  6.7 us
    dot_general x1, matrix products, per_device(): lax.dot_general(mine, cells, (((1,), (1,)), ((), ())), precision=PREC, pr...  4.41 us
    dot_general x1, matrix products, per_device(): lax.dot_general(zr, vd, (((1,), (1,)), ((), ())), precision=PREC, preferr...  4.35 us
  transfers between devices with their start and end apart: 9, of which 7 were waited for; matrix products, arithmetic and copies ran while one was open for 12% of the time, Pallas kernels for 0%

profile of v1, /device:TPU:1, one launch (start us, length us, event | category | flops | bytes accessed | tf_op | source)
XLA Modules:
  0.0 215.7 jit_solution(13416404276061215988)
XLA Ops:
  7.2 0.0 copy-start.3
  7.2 2.3 %copy.66 = f32[128,8,2,128]{0,3,2,1:T(8,128)} copy(f32[128,8,2,128]{3,2,1,0:T(2,128)} %param.3) | data formatting | bytes 2097152 | tf_op args[0]
  9.5 7.7 %all-to-all-start = ((f32[8,2,128,128]{2,3,1,0:T(8,128)}), f32[8,2,128,128]{2,3,1,0:T(8,128)S(1)}, u32[]{:S(2)}, u32[]{:S(2)}) async-start(f32[8,2,128,128]{2,3,1,0:T(8,128)} %bitcast), calls=%async_computation | async-start | bytes 2097152 | tf_op jit(solution)/shard_map/all_to_all | solution.py:12
  17.1 0.0 all-gather.3.cloned.1.call-start
  17.2 0.7 all-gather.3.cloned.1.call-update
  17.9 0.0 copy-done.3
  17.9 0.1 copy.74
  18.0 26.3 %all-to-all-done = f32[8,2,128,128]{2,3,1,0:T(8,128)S(1)} async-done(((f32[8,2,128,128]{2,3,1,0:T(8,128)}), f32[8,2,128,128]{2,3,1,0:T(8,128)S(1)}, u32[]{:S(2)}, u32[]{:S(2)}) %all-to-all-start) | async-done | bytes 1048608 | tf_op jit(solution)/shard_map/all_to_all | solution.py:12
  44.3 19.7 %all-gather.3.cloned.1.call-done = f32[1024,256]{1,0:T(8,128)} async-done(((f32[128,256]{1,0:T(8,128)}), f32[1024,256]{1,0:T(8,128)}) %all-gather.3.cloned.1.call-update) | async-done | bytes 1048592 | tf_op jit(solution)/shard_map/all_gather | solution.py:21
  64.0 1.8 convolution_bitcast_fusion
  65.9 0.1 copy.73
  66.0 0.1 broadcast_in_dim.11
  66.1 1.1 pad_maximum_fusion
  67.1 5.4 %all-to-all-start.2 = ((f32[4,544,128]{2,1,0:T(8,128)}), f32[4,544,128]{2,1,0:T(8,128)S(1)}, u32[]{:S(2)}, u32[]{:S(2)}) async-start(f32[4,544,128]{2,1,0:T(8,128)} %pad_maximum_fusion), calls=%async_computation.2 | async-start | bytes 2228224 | tf_op jit(solution)/shard_map/all_to_all | solution.py:12
  72.5 6.7 %collective-permute-start = (f32[8,2,128,128]{2,3,1,0:T(8,128)S(1)}, f32[8,2,128,128]{2,3,1,0:T(8,128)}, u32[]{:S(2)}, u32[]{:S(2)}) collective-permute-start(f32[8,2,128,128]{2,3,1,0:T(8,128)S(1)} %all-to-all-done), channel_id=1, source_target_pairs={{0,1},{1,0},{2,3},{3,2},{4,5},{5,4},{6,7},{7,6},{8,9},{9,8},{10,11... | collective-permute-start | bytes 3145736 | tf_op jit(solution)/shard_map/ppermute | solution.py:50
  79.3 0.6 copy.67
  79.9 1.8 concatenate.16
  81.7 0.8 copy.77
  82.6 0.0 collective-permute-done
  82.6 1.6 copy.68
  84.2 1.8 concatenate.17
  86.0 1.3 fusion.4
  87.3 1.0 copy.69
  88.3 1.5 copy_bitcast_fusion
  89.8 8.1 %all-to-all-done.2 = f32[4,544,128]{2,1,0:T(8,128)S(1)} async-done(((f32[4,544,128]{2,1,0:T(8,128)}), f32[4,544,128]{2,1,0:T(8,128)S(1)}, u32[]{:S(2)}, u32[]{:S(2)}) %all-to-all-start.2) | async-done | bytes 1114144 | tf_op jit(solution)/shard_map/all_to_all | solution.py:12
  97.9 1.1 fusion.8
  99.0 0.0 copy-start.2
  99.0 1.6 copy.78
  100.6 2.8 %reshape.104 = f32[512,512,1]{1,0,2:T(8,128)} reshape(f32[512,4,128]{2,1,0:T(4,128)} %copy.78) | data formatting | bytes 2097152 | tf_op jit(solution)/shard_map/reshape | solution.py:38
  103.5 0.0 copy-done.2
  103.5 2.3 %fusion.10 = f32[8,16,512]{2,1,0:T(8,128)} fusion(f32[8,16,512]{2,1,0:T(8,128)S(1)} %bitcast.84, f32[512,512,1]{1,0,2:T(8,128)} %reshape.104), kind=kOutput, calls=%fused_computation.27 | convolution fusion | flops 201326592 | bytes 1572864 | tf_op jit(solution)/shard_map/dot_general | solution.py:37
  105.8 7.0 %all-to-all-start.3 = ((f32[8,16,512]{2,1,0:T(8,128)}), f32[8,16,512]{2,1,0:T(8,128)S(1)}, u32[]{:S(2)}, u32[]{:S(2)}) async-start(f32[8,16,512]{2,1,0:T(8,128)} %fusion.10), calls=%async_computation.3 | async-start | bytes 524288 | tf_op jit(solution)/shard_map/all_to_all | solution.py:12
  112.8 0.0 copy-done
  112.9 0.0 copy-done.1
  112.9 4.4 %fusion = f32[4,128,1024]{2,1,0:T(8,128)} fusion(f32[4,128,512]{2,1,0:T(8,128)S(1)} %bitcast.74, f32[1024,256]{1,0:T(8,128)S(1)} %copy-done.1, f32[1024,256]{1,0:T(8,128)} %get-tuple-element.15), kind=kOutput, calls=%fused_computation.3 | convolution fusion | flops 1611137024 | bytes 5242880 | tf_op jit(solution)/shard_map/dot_general | solution.py:59
  117.3 2.1 all-to-all-done.3
  119.4 3.6 %all-to-all-start.1 = ((f32[4,128,1024]{2,1,0:T(8,128)}), f32[4,128,1024]{2,1,0:T(8,128)S(1)}, u32[]{:S(2)}, u32[]{:S(2)}) async-start(f32[4,128,1024]{2,1,0:T(8,128)} %fusion), calls=%async_computation.1 | async-start | bytes 4194304 | tf_op jit(solution)/shard_map/all_to_all | solution.py:12
  123.0 2.3 %copy.75 = f32[8,2,8,4,4,128]{5,2,4,3,1,0:T(8,128)} copy(f32[8,2,8,4,4,128]{5,2,3,0,1,4:T(8,128)} %bitcast.73) | data formatting | bytes 2097152 | tf_op jit(solution)/shard_map/transpose | solution.py:43
  125.4 0.2 broadcast_multiply_fusion
  125.6 1.4 reshape.103
  127.0 4.4 %fusion.9 = f32[8,16,128]{1,2,0:T(8,128)} fusion(f32[8,16,2048]{2,1,0:T(8,128)} %bitcast.80, f32[128,2048,1]{1,0,2:T(8,128)} %reshape.103), kind=kOutput, calls=%fused_computation.26 | convolution fusion | flops 201326592 | bytes 2162688 | tf_op jit(solution)/shard_map/dot_general | solution.py:46
  131.4 0.1 copy.80
  131.5 16.7 %all-to-all-done.1 = f32[4,128,1024]{2,1,0:T(8,128)S(1)} async-done(((f32[4,128,1024]{2,1,0:T(8,128)}), f32[4,128,1024]{2,1,0:T(8,128)S(1)}, u32[]{:S(2)}, u32[]{:S(2)}) %all-to-all-start.1) | async-done | bytes 2097184 | tf_op jit(solution)/shard_map/all_to_all | solution.py:12
  148.3 0.2 reduce_sum.45
  148.4 0.2 copy.72
  148.7 1.3 pad_maximum_fusion.1
  149.9 0.3 copy.82
  150.3 25.3 %all_to_all.35 = f32[8,208,128]{2,1,0:T(8,128)S(1)} all-to-all(f32[8,208,128]{2,1,0:T(8,128)S(1)} %copy.82), channel_id=1, replica_groups=mesh['y'=8,'zl'=4,'zh'=2,'x'=4,'c'=2] {'y'}, dimensions={0} | all-to-all | bytes 1703936 | tf_op jit(solution)/shard_map/all_to_all | solution.py:12
  175.5 0.7 slice_reduce_fusion
  176.2 6.1 %all-to-all-start.5 = ((f32[8,16,128]{2,1,0:T(8,128)}), f32[8,16,128]{2,1,0:T(8,128)S(1)}, u32[]{:S(2)}, u32[]{:S(2)}) async-start(f32[8,16,128]{2,1,0:T(8,128)} %bitcast.27), calls=%async_computation.5 | async-start | bytes 131072 | tf_op jit(solution)/shard_map/all_to_all | solution.py:12
  182.4 0.1 copy.93
  182.5 7.3 %collective-permute-start.1 = (f32[64,128]{0,1:T(8,128)S(1)}, f32[64,128]{0,1:T(8,128)S(1)}, u32[]{:S(2)}, u32[]{:S(2)}) collective-permute-start(f32[64,128]{0,1:T(8,128)S(1)} %copy.93), channel_id=1, source_target_pairs={{0,8},{8,0},{1,9},{9,1},{2,10},{10,2},{3,11},{11,3},{4,12},{12,4},... | collective-permute-start | bytes 98312 | tf_op jit(solution)/shard_map/ppermute | solution.py:76
  189.7 2.1 collective-permute-done.1
  191.8 0.1 copy.86
  191.9 0.0 all-to-all-done.5
  191.9 0.7 broadcast_in_dim.13
  192.6 8.8 %all-to-all-start.6 = ((f32[8,64,128]{2,1,0:T(8,128)}), f32[8,64,128]{2,1,0:T(8,128)S(1)}, u32[]{:S(2)}, u32[]{:S(2)}) async-start(f32[8,64,128]{2,1,0:T(8,128)} %broadcast_in_dim.13), calls=%async_computation.6 | async-start | bytes 524288 | tf_op jit(solution)/shard_map/all_to_all | solution.py:12
  201.5 0.2 reshape.97
  201.6 0.2 copy.88
  201.8 0.8 copy.89
  202.6 0.6 multiply_bitcast_fusion
  203.2 4.7 %all-to-all-done.6 = f32[8,64,128]{2,1,0:T(8,128)S(1)} async-done(((f32[8,64,128]{2,1,0:T(8,128)}), f32[8,64,128]{2,1,0:T(8,128)S(1)}, u32[]{:S(2)}, u32[]{:S(2)}) %all-to-all-start.6) | async-done | bytes 262176 | tf_op jit(solution)/shard_map/all_to_all | solution.py:12
  208.0 0.1 copy.87
  208.1 0.7 copy.100
  (14 shorter events, 0.2 us)
Async XLA Ops:
  7.2 10.7 %copy-start.3 = (f32[128,128]{1,0:T(8,128)S(1)}, f32[128,128]{1,0:T(8,128)}, u32[]{:S(2)}) copy-start(f32[128,128]{1,0:T(8,128)} %param.5) | copy-start | bytes 196612
  9.5 34.8 %all-to-all-start = ((f32[8,2,128,128]{2,3,1,0:T(8,128)}), f32[8,2,128,128]{2,3,1,0:T(8,128)S(1)}, u32[]{:S(2)}, u32[]{:S(2)}) async-start(f32[8,2,128,128]{2,3,1,0:T(8,128)} %bitcast), calls=%async_computation | async-start | bytes 2097152 | tf_op jit(solution)/shard_map/all_to_all | solution.py:12
  17.1 46.9 %all-gather.3.cloned.1.call-start = ((), (), s32[]{:S(2)}) async-start(), calls=%async_computation.7 | async-start | bytes 1179648 | tf_op jit(solution)/shard_map/all_gather | solution.py:21
  67.1 30.7 %all-to-all-start.2 = ((f32[4,544,128]{2,1,0:T(8,128)}), f32[4,544,128]{2,1,0:T(8,128)S(1)}, u32[]{:S(2)}, u32[]{:S(2)}) async-start(f32[4,544,128]{2,1,0:T(8,128)} %pad_maximum_fusion), calls=%async_computation.2 | async-start | bytes 2228224 | tf_op jit(solution)/shard_map/all_to_all | solution.py:12
  72.5 10.0 %collective-permute-start = (f32[8,2,128,128]{2,3,1,0:T(8,128)S(1)}, f32[8,2,128,128]{2,3,1,0:T(8,128)}, u32[]{:S(2)}, u32[]{:S(2)}) collective-permute-start(f32[8,2,128,128]{2,3,1,0:T(8,128)S(1)} %all-to-all-done), channel_id=1, source_target_pairs={{0,1},{1,0},{2,3},{3,2},{4,5},{5,4},{6,7},{7,6},{8,9},{9,8},{10,11... | collective-permute-start | bytes 3145736 | tf_op jit(solution)/shard_map/ppermute | solution.py:50
  99.0 4.5 %copy-start.2 = (f32[128,512]{1,0:T(8,128)S(1)}, f32[128,512]{1,0:T(8,128)}, u32[]{:S(2)}) copy-start(f32[128,512]{1,0:T(8,128)} %copy.77) | copy-start | bytes 786436
  100.6 12.2 %copy-start = (f32[4,8,16,512]{3,2,1,0:T(8,128)S(1)}, f32[4,8,16,512]{3,2,1,0:T(8,128)}, u32[]{:S(2)}) copy-start(f32[4,8,16,512]{3,2,1,0:T(8,128)} %copy.69) | copy-start | bytes 3145732
  100.6 12.2 %copy-start.1 = (f32[1024,256]{1,0:T(8,128)S(1)}, f32[1024,256]{1,0:T(8,128)}, u32[]{:S(2)}) copy-start(f32[1024,256]{1,0:T(8,128)} %get-tuple-element.14) | copy-start | bytes 3145732
  105.8 13.5 %all-to-all-start.3 = ((f32[8,16,512]{2,1,0:T(8,128)}), f32[8,16,512]{2,1,0:T(8,128)S(1)}, u32[]{:S(2)}, u32[]{:S(2)}) async-start(f32[8,16,512]{2,1,0:T(8,128)} %fusion.10), calls=%async_computation.3 | async-start | bytes 524288 | tf_op jit(solution)/shard_map/all_to_all | solution.py:12
  119.4 28.9 %all-to-all-start.1 = ((f32[4,128,1024]{2,1,0:T(8,128)}), f32[4,128,1024]{2,1,0:T(8,128)S(1)}, u32[]{:S(2)}, u32[]{:S(2)}) async-start(f32[4,128,1024]{2,1,0:T(8,128)} %fusion), calls=%async_computation.1 | async-start | bytes 4194304 | tf_op jit(solution)/shard_map/all_to_all | solution.py:12
  176.2 15.7 %all-to-all-start.5 = ((f32[8,16,128]{2,1,0:T(8,128)}), f32[8,16,128]{2,1,0:T(8,128)S(1)}, u32[]{:S(2)}, u32[]{:S(2)}) async-start(f32[8,16,128]{2,1,0:T(8,128)} %bitcast.27), calls=%async_computation.5 | async-start | bytes 131072 | tf_op jit(solution)/shard_map/all_to_all | solution.py:12
  182.5 9.4 %collective-permute-start.1 = (f32[64,128]{0,1:T(8,128)S(1)}, f32[64,128]{0,1:T(8,128)S(1)}, u32[]{:S(2)}, u32[]{:S(2)}) collective-permute-start(f32[64,128]{0,1:T(8,128)S(1)} %copy.93), channel_id=1, source_target_pairs={{0,8},{8,0},{1,9},{9,1},{2,10},{10,2},{3,11},{11,3},{4,12},{12,4},... | collective-permute-start | bytes 98312 | tf_op jit(solution)/shard_map/ppermute | solution.py:76
  192.6 15.3 %all-to-all-start.6 = ((f32[8,64,128]{2,1,0:T(8,128)}), f32[8,64,128]{2,1,0:T(8,128)S(1)}, u32[]{:S(2)}, u32[]{:S(2)}) async-start(f32[8,64,128]{2,1,0:T(8,128)} %broadcast_in_dim.13), calls=%async_computation.6 | async-start | bytes 524288 | tf_op jit(solution)/shard_map/all_to_all | solution.py:12
Sparse Core Ops, SparseCore 0:
  20.1 43.9 all-gather.2

commit v2 on v1

v2 whole, which is shorter than its diff:
```python
import jax
import jax.numpy as jnp
from jax import lax
from jax.sharding import Mesh
from jax.sharding import PartitionSpec as P

NY, NZL, NZH, NX, NC = 8, 4, 2, 4, 2
PREC = lax.Precision.HIGH


def exchange(a, axes):
    return lax.all_to_all(a, axes, 0, 0)


def dot(a, b, dims):
    return lax.dot_general(a, b, (dims, ((), ())), precision=PREC, preferred_element_type=jnp.float32)


def per_device(field, u, v):
    f32 = jnp.float32
    core_id = lax.axis_index("c")
    x_id = lax.axis_index("x")

    u_half = lax.dynamic_slice_in_dim(u, 128 * core_id, 128, 1)
    send = jnp.concatenate(
        [jnp.transpose(field, (1, 2, 0, 3)), jnp.broadcast_to(u_half, (NY, 1, 128, 128))], axis=1
    )
    own = exchange(send, "y")
    other = lax.ppermute(own, "c", [(0, 1), (1, 0)])

    f = own[:, :2]
    z = jnp.concatenate(
        [dot(own[:, 2], f, ((0, 1), (0, 2))), dot(other[:, 2], f, ((0, 1), (0, 2)))], axis=0
    ).reshape(512, 128)

    vt = jnp.transpose(v).reshape(NZL, 32, 128)
    zv = jnp.concatenate([jnp.broadcast_to(z, (NZL, 512, 128)), vt], axis=1)
    zv = exchange(zv, "zl")
    zg, vg = zv[:, :512], zv[:, 512:]

    def rows_of(a):
        return jnp.transpose(a[:, :2], (0, 2, 1, 3)).reshape(1024, 256)

    cells = jnp.concatenate([rows_of(own), rows_of(other)], axis=1)
    mine = cells.reshape(8, 4, 2, 16, 512)
    mine = lax.dynamic_index_in_dim(mine, core_id, 2, keepdims=False)
    mine = jnp.transpose(mine, (1, 0, 2, 3)).reshape(512, 512)
    g1 = dot(mine, cells, ((1,), (1,))).reshape(NX, 128, 1024)
    total = lax.dynamic_index_in_dim(g1, x_id, 0, keepdims=False)
    for d in (2, 1, 3):
        piece = lax.dynamic_index_in_dim(g1, (x_id + d) % NX, 0, keepdims=False)
        total = total + lax.ppermute(piece, "x", [(i, (i + d) % NX) for i in range(NX)])
    g1 = jnp.transpose(total.reshape(128, 8, 128), (1, 0, 2))

    g2 = dot(z, jnp.transpose(zg, (1, 0, 2)).reshape(512, 512), ((0,), (0,)))
    g2 = jnp.sum(exchange(g2.reshape(8, 16, 512), ("x", "c")), axis=0)
    g2 = jnp.transpose(g2.reshape(16, 4, 128), (1, 0, 2)).reshape(64, 128)

    zr = zg.reshape(NZL, 8, 4, 16, 128)
    zr = jnp.transpose(zr, (1, 3, 2, 0, 4)).reshape(128, 4 * 512)
    vd = jnp.eye(4, dtype=f32)[:, None, :, None, None] * jnp.transpose(vg, (1, 0, 2))[None, :, None]
    core_rows = dot(zr, vd.reshape(128, 4 * 512), ((1,), (1,))).reshape(8, 16, 128)
    core_rows = jnp.where(core_id == 0, core_rows, jnp.roll(core_rows, 4, axis=0))

    send = jnp.concatenate([g1, core_rows, jnp.broadcast_to(g2, (8, 64, 128))], axis=1)
    got = exchange(send, "y")
    core = got[:, 128:144].reshape(8, 8, 2, 4, 32)
    core = jnp.transpose(core, (3, 1, 0, 2, 4)).reshape(32, 8, 2, 32)
    g1 = jnp.sum(got[:, :128], axis=0).reshape(8, 16, 128)
    g2 = jnp.sum(got[:, 144:], axis=0)

    got = exchange(jnp.concatenate([g1, jnp.broadcast_to(g2, (8, 64, 128))], axis=1), ("zl", "zh"))
    gram_one = jnp.transpose(jnp.sum(got[:, :16], axis=0)) / 131072.0
    zl_id = lax.axis_index("zl")
    g2 = jnp.sum(lax.dynamic_slice_in_dim(got, 2 * zl_id, 2, 0)[:, 16:], axis=0)
    g2 = exchange(jnp.broadcast_to(g2, (8, 64, 128)), ("x", "c"))
    g2 = jnp.transpose(g2.reshape(8, 4, 16, 128), (0, 2, 1, 3)).reshape(128, 512)
    gram_two = g2 / 65536.0
    return gram_one, gram_two, core


def solution(mesh):
    split = Mesh(mesh.devices.reshape(NY, NZL, NZH, NX, NC), ("y", "zl", "zh", "x", "c"))
    gz = ("zh", "x", "c")
    return jax.shard_map(
        per_device,
        mesh=split,
        in_specs=(P("y", None, gz, "zl"), P("y", None), P("zl", None)),
        out_specs=(P("y", ("zl",) + gz), P("zl", None), P("y", None, gz, "zl")),
        check_vma=False,
    )
```

time: 217 us -> 188 us (0.87)
  waiting for transfers between devices: 80.4 us -> 35.6 us
  blocking collectives: 25.3 us -> 69.9 us
  between operations: 14.3 us -> 1.12 us
  starting transfers between devices: 52.7 us -> 44.1 us
  matrix products: 12.9 us -> 6.54 us
    all_to_all x1 -> x2, blocking collectives: 25.3 us -> 69.9 us  [exchange(): return lax.all_to_all(a, axes, 0, 0)]
    all_to_all x6 -> x4, waiting for transfers between devices: 58 us -> 14.7 us  [exchange(): return lax.all_to_all(a, axes, 0, 0)]
    all_gather x1 -> x0, waiting for transfers between devices: 19.7 us -> none  [per_device(): u_all = lax.all_gather(u, 'y', axis=0)]
    ppermute x2 -> x4, waiting for transfers between devices: 2.08 us -> 20.9 us  [the longest x3 20.9 us: per_device(): lax.ppermute(piece, 'x', [(i, (i + d) % NX) for i in range(NX)])]
    all_to_all x6 -> x4, starting transfers between devices: 38.6 us -> 28.5 us  [exchange(): return lax.all_to_all(a, axes, 0, 0)]
    dot_general x4 -> x5, matrix products: 12.9 us -> 6.54 us  [dot(): lax.dot_general(a, b, (dims, ((), ())), precision=PREC, preferred_element...]
    reshape x3 -> x5, local copies, waits for them, and re-layouts: 4.46 us -> 1.34 us  [the longest x1 0.42 us: per_device(): zr = jnp.transpose(zr, (1, 3, 2, 0, 4)).reshape(128, 4 * 512)]
    ppermute x2 -> x4, starting transfers between devices: 14 us -> 15.6 us  [the longest x3 9.92 us: per_device(): lax.ppermute(piece, 'x', [(i, (i + d) % NX) for i in range(NX)])]
  transfers between devices with their start and end apart: 9 -> 8, of which waited for: 7 -> 5; matrix products, arithmetic and copies ran while one was open for 12% -> 12% of each run, Pallas kernels for 0% -> 0%
where the time goes in v2:
time: 188 us; the launch traced here: 186 us
  blocking collectives  69.9 us (37%)
  starting transfers between devices  44.1 us (23%)
  waiting for transfers between devices  35.6 us (19%)
  local copies, waits for them, and re-layouts  23 us (12%)
  matrix products  6.54 us (3%)
  other arithmetic  6 us (3%)
    all_to_all x2, blocking collectives, exchange(): return lax.all_to_all(a, axes, 0, 0)  69.9 us
    all_to_all x4, starting transfers between devices, exchange(): return lax.all_to_all(a, axes, 0, 0)  28.5 us
    ppermute x3, waiting for transfers between devices, per_device(): lax.ppermute(piece, 'x', [(i, (i + d) % NX) for i in range(NX)])  20.9 us
    all_to_all x4, waiting for transfers between devices, exchange(): return lax.all_to_all(a, axes, 0, 0)  14.7 us
    ppermute x3, starting transfers between devices, per_device(): lax.ppermute(piece, 'x', [(i, (i + d) % NX) for i in range(NX)])  9.92 us
    dot_general x5, matrix products, dot(): lax.dot_general(a, b, (dims, ((), ())), precision=PREC, preferred_element...  6.54 us
    ppermute x1, starting transfers between devices, per_device(): other = lax.ppermute(own, 'c', [(0, 1), (1, 0)])  5.64 us
    transpose x4, local copies, waits for them, and re-layouts, rows_of(): return jnp.transpose(a[:, :2], (0, 2, 1, 3)).reshape(1024, 256)  4.8 us
  transfers between devices with their start and end apart: 8, of which 5 were waited for; matrix products, arithmetic and copies ran while one was open for 12% of the time, Pallas kernels for 0%

profile of v2, /device:TPU:1, one launch (start us, length us, event | category | flops | bytes accessed | tf_op | source)
XLA Modules:
  0.0 186.3 jit_solution(18305659955485330175)
XLA Ops:
  0.6 0.0 copy-start
  0.7 1.6 copy.169
  2.3 0.1 pad_maximum_fusion
  2.5 44.6 %all_to_all.30 = f32[8,3,128,128]{3,2,1,0:T(8,128)S(1)} all-to-all(f32[8,3,128,128]{3,2,1,0:T(8,128)S(1)} %pad_maximum_fusion), channel_id=1, replica_groups=mesh['y'=8,'zl'=4,'zh'=2,'x'=4,'c'=2] {'y'}, dimensions={0} | all-to-all | bytes 3145728 | tf_op jit(solution)/shard_map/all_to_all | solution.py:12
  47.1 1.6 copy.131
  48.7 5.6 %collective-permute-start = (f32[8,3,128,128]{2,3,0,1:T(8,128)}, f32[8,3,128,128]{2,3,0,1:T(8,128)}, u32[]{:S(2)}, u32[]{:S(2)}) collective-permute-start(f32[8,3,128,128]{2,3,0,1:T(8,128)} %copy.131), channel_id=1, source_target_pairs={{0,1},{1,0},{2,3},{3,2},{4,5},{5,4},{6,7},{7,6},{8,9},{9,8},{10,11... | collective-permute-start | bytes 4718600 | tf_op jit(solution)/shard_map/ppermute | solution.py:29
  54.4 0.1 copy.139
  54.5 0.1 slice_bitcast_fusion.1
  54.6 0.8 copy.130
  55.5 1.8 concatenate.30
  57.3 1.4 convolution_bitcast_fusion.1
  58.7 1.4 convolution_bitcast_fusion
  60.2 0.2 copy.138
  60.4 0.1 broadcast_in_dim.18
  60.5 1.1 pad_maximum_fusion.1
  61.6 7.0 %all-to-all-start.1 = ((f32[4,544,128]{2,1,0:T(8,128)}), f32[4,544,128]{2,1,0:T(8,128)}, u32[]{:S(2)}, u32[]{:S(2)}) async-start(f32[4,544,128]{2,1,0:T(8,128)} %pad_maximum_fusion.1), calls=%async_computation.1 | async-start | bytes 2228224 | tf_op jit(solution)/shard_map/all_to_all | solution.py:12
  68.6 2.3 %slice_bitcast_fusion = f32[8,128,2,128]{1,3,0,2:T(8,128)} fusion(f32[8,3,128,128]{2,3,0,1:T(8,128)} %collective-permute-done), kind=kLoop, calls=%fused_computation.14 | loop fusion | bytes 2097152 | tf_op jit(solution)/shard_map/transpose | solution.py:42
  70.9 1.6 copy.132
  72.5 1.8 concatenate.31
  74.3 1.3 fusion.4
  75.6 0.1 copy.133
  75.7 0.1 copy_bitcast_fusion
  75.9 1.9 %fusion = f32[4,128,1024]{2,1,0:T(8,128)S(1)} fusion(f32[4,128,512]{2,1,0:T(8,128)S(1)} %bitcast.102, f32[1024,256]{1,0:T(8,128)S(1)} %get-tuple-element.25, f32[1024,256]{1,0:T(8,128)S(1)} %get-tuple-element.26), kind=kOutput, calls=%fused_computation.3 | convolution fusion | flops 1611137024 | bytes 5242880 | tf_op jit(solution)/shard_map/dot_general | solution.py:16
  77.8 1.1 dynamic-slice_bitcast_fusion.2
  78.9 4.4 %collective-permute-start.3 = (f32[128,1024]{1,0:T(8,128)}, f32[128,1024]{1,0:T(8,128)}, u32[]{:S(2)}, u32[]{:S(2)}) collective-permute-start(f32[128,1024]{1,0:T(8,128)} %get-tuple-element.19), channel_id=1, source_target_pairs={{0,6},{2,0},{4,2},{6,4},{1,7},{3,1},{5,3},{7,5},{8,14},{10,8},{12,... | collective-permute-start | bytes 1572872 | tf_op jit(solution)/shard_map/ppermute | solution.py:52
  83.3 1.9 %collective-permute-start.2 = (f32[128,1024]{1,0:T(8,128)}, f32[128,1024]{1,0:T(8,128)}, u32[]{:S(2)}, u32[]{:S(2)}) collective-permute-start(f32[128,1024]{1,0:T(8,128)} %get-tuple-element.20), channel_id=1, source_target_pairs={{0,2},{2,4},{4,6},{6,0},{1,3},{3,5},{5,7},{7,1},{8,10},{10,12},{12... | collective-permute-start | bytes 1572872 | tf_op jit(solution)/shard_map/ppermute | solution.py:52
  85.2 3.6 %collective-permute-start.1 = (f32[128,1024]{1,0:T(8,128)S(1)}, f32[128,1024]{1,0:T(8,128)}, u32[]{:S(2)}, u32[]{:S(2)}) collective-permute-start(f32[128,1024]{1,0:T(8,128)S(1)} %get-tuple-element.18), channel_id=1, source_target_pairs={{0,4},{2,6},{4,0},{6,2},{1,5},{3,7},{5,1},{7,3},{8,12},{10,14},{12... | collective-permute-start | bytes 1572872 | tf_op jit(solution)/shard_map/ppermute | solution.py:52
  88.9 0.1 copy.144
  89.0 16.7 %collective-permute-done.3 = f32[128,1024]{1,0:T(8,128)} collective-permute-done((f32[128,1024]{1,0:T(8,128)}, f32[128,1024]{1,0:T(8,128)}, u32[]{:S(2)}, u32[]{:S(2)}) %collective-permute-start.3) | collective-permute-done | bytes 524320 | tf_op jit(solution)/shard_map/ppermute | solution.py:52
  105.7 4.2 %collective-permute-done.1 = f32[128,1024]{1,0:T(8,128)} collective-permute-done((f32[128,1024]{1,0:T(8,128)S(1)}, f32[128,1024]{1,0:T(8,128)}, u32[]{:S(2)}, u32[]{:S(2)}) %collective-permute-start.1) | collective-permute-done | bytes 524320 | tf_op jit(solution)/shard_map/ppermute | solution.py:52
  110.0 1.5 fusion.8
  111.5 1.0 copy.136
  112.5 0.0 all-to-all-done.1
  112.5 1.4 fusion.11
  113.8 0.7 copy.145
  114.5 0.4 reshape.108
  114.9 1.1 fusion.14
  116.1 5.7 %all-to-all-start.2 = ((f32[8,16,512]{2,1,0:T(8,128)}), f32[8,16,512]{2,1,0:T(8,128)S(1)}, u32[]{:S(2)}, u32[]{:S(2)}) async-start(f32[8,16,512]{2,1,0:T(8,128)} %fusion.14), calls=%async_computation.2 | async-start | bytes 524288 | tf_op jit(solution)/shard_map/all_to_all | solution.py:12
  121.7 0.7 copy.140
  122.4 0.4 reshape.95
  122.8 0.9 slice_bitcast_fusion.6
  123.7 0.2 broadcast_multiply_fusion
  124.0 0.4 mul.29
  124.4 0.6 fusion.13
  125.0 0.2 copy.142
  125.2 0.2 copy.143
  125.4 0.1 broadcast_select_fusion
  125.5 2.7 %all-to-all-done.2 = f32[8,16,512]{2,1,0:T(8,128)S(1)} async-done(((f32[8,16,512]{2,1,0:T(8,128)}), f32[8,16,512]{2,1,0:T(8,128)S(1)}, u32[]{:S(2)}, u32[]{:S(2)}) %all-to-all-start.2) | async-done | bytes 262176 | tf_op jit(solution)/shard_map/all_to_all | solution.py:12
  128.3 0.1 copy.147
  128.4 0.2 pad_maximum_fusion.2
  128.7 0.3 copy.148
  129.0 25.3 %all_to_all.31 = f32[8,208,128]{2,1,0:T(8,128)S(1)} all-to-all(f32[8,208,128]{2,1,0:T(8,128)S(1)} %copy.148), channel_id=1, replica_groups=mesh['y'=8,'zl'=4,'zh'=2,'x'=4,'c'=2] {'y'}, dimensions={0} | all-to-all | bytes 1703936 | tf_op jit(solution)/shard_map/all_to_all | solution.py:12
  154.4 0.7 pad_maximum_fusion.3
  155.1 7.6 %all-to-all-start.4 = ((f32[8,80,128]{2,1,0:T(8,128)}), f32[8,80,128]{2,1,0:T(8,128)S(1)}, u32[]{:S(2)}, u32[]{:S(2)}) async-start(f32[8,80,128]{2,1,0:T(8,128)} %pad_maximum_fusion.3), calls=%async_computation.4 | async-start | bytes 655360 | tf_op jit(solution)/shard_map/all_to_all | solution.py:12
  162.7 0.2 reshape.101
  162.9 0.2 copy.154
  163.0 0.8 copy.155
  163.9 6.0 %all-to-all-done.4 = f32[8,80,128]{2,1,0:T(8,128)S(1)} async-done(((f32[8,80,128]{2,1,0:T(8,128)}), f32[8,80,128]{2,1,0:T(8,128)S(1)}, u32[]{:S(2)}, u32[]{:S(2)}) %all-to-all-start.4) | async-done | bytes 327712 | tf_op jit(solution)/shard_map/all_to_all | solution.py:12
  169.9 0.7 broadcast_in_dim.21
  170.7 8.3 %all-to-all-start.5 = ((f32[8,64,128]{2,1,0:T(8,128)}), f32[8,64,128]{2,1,0:T(8,128)S(1)}, u32[]{:S(2)}, u32[]{:S(2)}) async-start(f32[8,64,128]{2,1,0:T(8,128)} %broadcast_in_dim.21), calls=%async_computation.5 | async-start | bytes 524288 | tf_op jit(solution)/shard_map/all_to_all | solution.py:12
  179.0 0.6 multiply_bitcast_fusion
  179.6 5.9 %all-to-all-done.5 = f32[8,64,128]{2,1,0:T(8,128)S(1)} async-done(((f32[8,64,128]{2,1,0:T(8,128)}), f32[8,64,128]{2,1,0:T(8,128)S(1)}, u32[]{:S(2)}, u32[]{:S(2)}) %all-to-all-start.5) | async-done | bytes 262176 | tf_op jit(solution)/shard_map/all_to_all | solution.py:12
  185.5 0.1 copy.153
  185.6 0.7 copy.170
  (25 shorter events, 0.3 us)
Async XLA Ops:
  0.6 1.6 copy-start
  47.1 7.3 %copy-start.2 = (f32[128,128]{1,0:T(8,128)S(1)}, f32[128,128]{1,0:T(8,128)}, u32[]{:S(2)}) copy-start(f32[128,128]{1,0:T(8,128)} %param.5) | copy-start | bytes 196612
  48.7 10.0 %collective-permute-start = (f32[8,3,128,128]{2,3,0,1:T(8,128)}, f32[8,3,128,128]{2,3,0,1:T(8,128)}, u32[]{:S(2)}, u32[]{:S(2)}) collective-permute-start(f32[8,3,128,128]{2,3,0,1:T(8,128)} %copy.131), channel_id=1, source_target_pairs={{0,1},{1,0},{2,3},{3,2},{4,5},{5,4},{6,7},{7,6},{8,9},{9,8},{10,11... | collective-permute-start | bytes 4718600 | tf_op jit(solution)/shard_map/ppermute | solution.py:29
  61.6 50.9 %all-to-all-start.1 = ((f32[4,544,128]{2,1,0:T(8,128)}), f32[4,544,128]{2,1,0:T(8,128)}, u32[]{:S(2)}, u32[]{:S(2)}) async-start(f32[4,544,128]{2,1,0:T(8,128)} %pad_maximum_fusion.1), calls=%async_computation.1 | async-start | bytes 2228224 | tf_op jit(solution)/shard_map/all_to_all | solution.py:12
  78.9 26.8 %collective-permute-start.3 = (f32[128,1024]{1,0:T(8,128)}, f32[128,1024]{1,0:T(8,128)}, u32[]{:S(2)}, u32[]{:S(2)}) collective-permute-start(f32[128,1024]{1,0:T(8,128)} %get-tuple-element.19), channel_id=1, source_target_pairs={{0,6},{2,0},{4,2},{6,4},{1,7},{3,1},{5,3},{7,5},{8,14},{10,8},{12,... | collective-permute-start | bytes 1572872 | tf_op jit(solution)/shard_map/ppermute | solution.py:52
  83.3 22.4 %collective-permute-start.2 = (f32[128,1024]{1,0:T(8,128)}, f32[128,1024]{1,0:T(8,128)}, u32[]{:S(2)}, u32[]{:S(2)}) collective-permute-start(f32[128,1024]{1,0:T(8,128)} %get-tuple-element.20), channel_id=1, source_target_pairs={{0,2},{2,4},{4,6},{6,0},{1,3},{3,5},{5,7},{7,1},{8,10},{10,12},{12... | collective-permute-start | bytes 1572872 | tf_op jit(solution)/shard_map/ppermute | solution.py:52
  85.2 24.7 %collective-permute-start.1 = (f32[128,1024]{1,0:T(8,128)S(1)}, f32[128,1024]{1,0:T(8,128)}, u32[]{:S(2)}, u32[]{:S(2)}) collective-permute-start(f32[128,1024]{1,0:T(8,128)S(1)} %get-tuple-element.18), channel_id=1, source_target_pairs={{0,4},{2,6},{4,0},{6,2},{1,5},{3,7},{5,1},{7,3},{8,12},{10,14},{12... | collective-permute-start | bytes 1572872 | tf_op jit(solution)/shard_map/ppermute | solution.py:52
  116.1 12.2 %all-to-all-start.2 = ((f32[8,16,512]{2,1,0:T(8,128)}), f32[8,16,512]{2,1,0:T(8,128)S(1)}, u32[]{:S(2)}, u32[]{:S(2)}) async-start(f32[8,16,512]{2,1,0:T(8,128)} %fusion.14), calls=%async_computation.2 | async-start | bytes 524288 | tf_op jit(solution)/shard_map/all_to_all | solution.py:12
  125.2 3.2 %copy-start.1 = (f32[128,1024]{0,1:T(8,128)S(1)}, f32[128,1024]{0,1:T(8,128)}, u32[]{:S(2)}) copy-start(f32[128,1024]{0,1:T(8,128)} %copy.136) | copy-start | bytes 1572868
  155.1 14.8 %all-to-all-start.4 = ((f32[8,80,128]{2,1,0:T(8,128)}), f32[8,80,128]{2,1,0:T(8,128)S(1)}, u32[]{:S(2)}, u32[]{:S(2)}) async-start(f32[8,80,128]{2,1,0:T(8,128)} %pad_maximum_fusion.3), calls=%async_computation.4 | async-start | bytes 655360 | tf_op jit(solution)/shard_map/all_to_all | solution.py:12
  170.7 14.8 %all-to-all-start.5 = ((f32[8,64,128]{2,1,0:T(8,128)}), f32[8,64,128]{2,1,0:T(8,128)S(1)}, u32[]{:S(2)}, u32[]{:S(2)}) async-start(f32[8,64,128]{2,1,0:T(8,128)} %broadcast_in_dim.21), calls=%async_computation.5 | async-start | bytes 524288 | tf_op jit(solution)/shard_map/all_to_all | solution.py:12

commit v3 on v0

v3 whole, which is shorter than its diff:
```python
import jax
import jax.numpy as jnp
from jax import lax
from jax.experimental import pallas as pl
from jax.experimental.pallas import tpu as pltpu
from jax.sharding import Mesh
from jax.sharding import PartitionSpec as P

NY, NYL, NZL, NZH, NX, NC = 8, 4, 4, 2, 4, 2
Y = ("yh", "yl")
F32, BF16 = jnp.float32, jnp.bfloat16


def exchange(a, axes):
    return lax.all_to_all(a, axes, 0, 0)


def shift(a, axis, size, d):
    return lax.ppermute(a, axis, [(i, (i + d) % size) for i in range(size)])


def split(a):
    hi = a.astype(BF16)
    return hi, (a - hi.astype(F32)).astype(BF16)


def dot3(a, b, dims):
    def one(p, q):
        return lax.dot_general(p, q, (dims, ((), ())), preferred_element_type=F32)

    return one(a[0], b[0]) + (one(a[0], b[1]) + one(a[1], b[0]))


def project_kernel(ids, own, other, after, o0, o1, o2, o3, res):
    c = ids[1]
    total = [jnp.zeros((128, 256), F32)] * 2
    for y in range(NY):
        f = split(jnp.concatenate([own[y, 0], own[y, 1]], axis=1))
        for h, ref in enumerate((own, other)):
            total[h] += dot3(split(ref[y, 2]), f, ((0,), (0,)))
    for h in range(2):
        half = c if h == 0 else 1 - c
        for rg in range(4):
            k, first = rg // 2, 4 * (rg % 2)
            at = pl.multiple_of(32 * rg + 16 * half, 16)
            for g in range(4):
                rows = [
                    total[h][32 * yq + 8 * g + first : 32 * yq + 8 * g + first + 4, 128 * k : 128 * k + 128]
                    for yq in range(4)
                ]
                res[g, pl.ds(at, 16), :] = jnp.concatenate(rows, axis=0)
    for d, o in enumerate((o0, o1, o2, o3)):
        o[...] = res[lax.rem(ids[2] + d, NZL)]


def gram_one_kernel(ids, own, other, out, hi, lo, row_hi, row_lo):
    n = pl.program_id(0)

    @pl.when(n == 0)
    def _():
        for i, ref in enumerate((own, other)):
            for k in range(2):
                for y in range(NY):
                    col = 256 * i + 128 * k
                    a, b = split(ref[y, k])
                    hi[128 * y : 128 * y + 128, col : col + 128] = a
                    lo[128 * y : 128 * y + 128, col : col + 128] = b
        for x in range(NX):
            for b in range(8):
                src = pl.ds(pl.multiple_of(128 * b + 32 * x + 16 * ids[1], 16), 16)
                dst = slice(128 * x + 16 * b, 128 * x + 16 * b + 16)
                row_hi[dst, :] = hi[src, :]
                row_lo[dst, :] = lo[src, :]

    cols = pl.ds(pl.multiple_of(256 * n, 256), 256)
    r = dot3((row_hi[...], row_lo[...]), (hi[cols, :], lo[cols, :]), ((1,), (1,)))
    for x in range(NX):
        for y in range(2):
            for b in range(8):
                at = 128 * x + 16 * b
                out[x, 8 * y + b] = r[at : at + 16, 128 * y : 128 * y + 128]


def gram_two_kernel(ids, own, other, o0, o1, o2, o3, hi, lo, res):
    for n, ref in enumerate((own, other)):
        for b in range(4):
            rows = slice(128 * n, 128 * n + 128)
            cols = pl.ds(pl.multiple_of(128 * lax.rem(ids[2] + NZL - b, NZL), 128), 128)
            p, q = split(ref[b])
            hi[rows, cols] = p
            lo[rows, cols] = q
    cols = pl.ds(pl.multiple_of(256 * ids[1], 256), 256)
    res[...] = dot3((hi[...], lo[...]), (hi[:, cols], lo[:, cols]), ((0,), (0,)))
    for d, o in enumerate((o0, o1, o2, o3)):
        x = lax.rem(ids[0] + d, NX)
        for zl in range(NZL):
            part = res[pl.ds(pl.multiple_of(128 * zl + 32 * x, 32), 32), :]
            for yl in range(NYL):
                for lb in range(2):
                    o[NZL * (NYL * lb + yl) + zl] = part[8 * yl : 8 * yl + 8, 128 * lb : 128 * lb + 128]


def core_kernel(ids, z, v0, v1, v2, v3, out):
    lane = lax.broadcasted_iota(jnp.int32, (128, 128), 1)
    total = jnp.zeros((32, 512), F32)
    for n, v in enumerate((v0, v1, v2, v3)):
        zn, vn = z[n], v[...]
        moved = [vn] + [pltpu.roll(vn, 32 * d, 1) for d in range(1, 4)]
        for rg in range(4):
            here = (lane >= 32 * rg) & (lane < 32 * rg + 32)
            cols = [jnp.where(here, moved[(rg - zl) % 4], 0.0) for zl in range(NZL)]
            total += dot3(split(zn[32 * rg : 32 * rg + 32]), split(jnp.concatenate(cols, axis=1)), ((1,), (0,)))
    for y in range(NY):
        for zl in range(NZL):
            part = total[4 * y : 4 * y + 4, 128 * zl : 128 * zl + 128]
            out[y, zl] = jnp.concatenate([part, part], axis=0)


def call(kernel, out_shape, flops, *args, scratch=(), grid=None, out_specs=None, unread=0):
    vmem = pl.BlockSpec(memory_space=pltpu.VMEM)
    outs = jax.tree.map(lambda s: jax.ShapeDtypeStruct(s, F32), out_shape, is_leaf=lambda s: isinstance(s[0], int))
    kw = {} if grid is None else {"grid": grid}
    return pl.pallas_call(
        kernel,
        out_shape=outs,
        in_specs=[pl.BlockSpec(memory_space=pltpu.SMEM)] + [vmem] * (len(args) - 1 - unread)
        + [pl.BlockSpec(memory_space=pl.ANY)] * unread,
        out_specs=jax.tree.map(lambda _: vmem, outs) if out_specs is None else out_specs,
        scratch_shapes=list(scratch),
        compiler_params=pltpu.CompilerParams(vmem_limit_bytes=32 * 2**20),
        cost_estimate=pl.CostEstimate(flops=flops, bytes_accessed=4 * 2**20, transcendentals=0),
        **kw,
    )(*args)


def per_device(field, u, v):
    core_id, x_id, zl_id = lax.axis_index("c"), lax.axis_index("x"), lax.axis_index("zl")
    ids = jnp.stack([x_id, core_id, zl_id]).astype(jnp.int32)

    u_half = lax.dynamic_slice_in_dim(u, 128 * core_id, 128, 1)
    send = jnp.concatenate(
        [jnp.transpose(field, (1, 2, 0, 3)), jnp.broadcast_to(u_half, (NY, 1, 128, 128))], axis=1
    )
    own = exchange(send, Y)
    v_all = [v] + [shift(v, "zl", NZL, d) for d in range(1, NZL)]
    own, v_all = lax.optimization_barrier((own, v_all))
    other = lax.ppermute(own, "c", [(0, 1), (1, 0)])

    g1 = call(
        gram_one_kernel,
        (NX, 64, 16, 128),
        2 * 1024 * 512 * 512 * 3,
        ids,
        own,
        other,
        grid=(4,),
        out_specs=pl.BlockSpec((NX, 16, 16, 128), lambda n: (0, n, 0, 0)),
        scratch=[pltpu.VMEM((1024, 512), BF16)] * 2 + [pltpu.VMEM((512, 512), BF16)] * 2,
    )
    z = call(
        project_kernel,
        ((128, 128),) * 4,
        2 * 1024 * 256 * 256 * 3,
        ids,
        own,
        other,
        g1,
        unread=1,
        scratch=[pltpu.VMEM((NZL, 128, 128), F32)],
    )
    z = jnp.stack([z[0]] + [shift(z[d], "zl", NZL, d) for d in range(1, NZL)])

    z_other = lax.ppermute(z, "c", [(0, 1), (1, 0)])
    g2 = call(
        gram_two_kernel,
        ((32, 8, 128),) * 4,
        2 * 512 * 256 * 256 * 3,
        ids,
        z,
        z_other,
        scratch=[pltpu.VMEM((256, 512), BF16)] * 2 + [pltpu.VMEM((512, 256), F32)],
    )
    g2 = [g2[0]] + [shift(g2[d], "x", NX, d) for d in range(1, NX)]
    core = call(core_kernel, (NY, NZL, 8, 128), 2 * 128 * 512 * 512 * 3, ids, z, *v_all)

    g1 = jnp.sum(exchange(g1, "x"), axis=0)
    g2 = jnp.repeat(g2[0] + g2[1] + g2[2] + g2[3], NZH, axis=0)
    core = jnp.repeat(core.reshape(32, 8, 128), NZH, axis=0)
    got = exchange(jnp.concatenate([g1, g2, core], axis=1), Y + ("zl", "zh"))
    g2 = jnp.sum(got[:, 16:24], axis=0)
    g2 = exchange(jnp.broadcast_to(g2, (64, 8, 128)), Y + ("x", "c"))
    gram_one = jnp.transpose(jnp.sum(got[:, :16], axis=0)) / 131072.0
    core = lax.dynamic_index_in_dim(got.reshape(32, NZH, 32, 128), lax.axis_index("zh"), 1, keepdims=False)
    core = core[:, 24:28].reshape(8, 4, 4, 2, 2, 32)
    core = jnp.transpose(core, (1, 4, 2, 0, 3, 5)).reshape(32, 8, 2, 32)
    g2 = g2.reshape(2, NYL, NX, NC, 8, 128)
    g2 = jnp.transpose(g2, (2, 1, 4, 3, 0, 5)).reshape(128, 512)
    gram_two = g2 / 65536.0
    return gram_one, gram_two, core


def solution(mesh):
    by_axis = Mesh(mesh.devices.reshape(2, NYL, NZL, NZH, NX, NC), Y + ("zl", "zh", "x", "c"))
    gz = ("zh", "x", "c")
    return jax.shard_map(
        per_device,
        mesh=by_axis,
        in_specs=(P(Y, None, gz, "zl"), P(Y, None), P("zl", None)),
        out_specs=(P(Y, ("zl",) + gz), P("zl", None), P(Y, None, gz, "zl")),
        check_vma=False,
    )
```

time: 2010 us -> 166 us (0.08)
  waiting for transfers between devices: 1940 us -> 46.9 us
  starting transfers between devices: 0.43 us -> 65.4 us
  blocking collectives: 0 us -> 35.1 us
    psum x1 -> x0, waiting for transfers between devices: 1430 us -> none  [per_device(): gram_two = lax.psum(gram_terms, ('gx', 'gz')) / (R1 * third_total * levels)]
    reduce_scatter x2 -> x0, waiting for transfers between devices: 370 us -> none  [the longest x1 324 us: per_device(): lax.psum_scatter(block, ('gy', 'gz'), scatter_dimension=1, tiled=True)]
    all_gather x2 -> x0, waiting for transfers between devices: 122 us -> none  [the longest x1 93.2 us: per_device(): piece = lax.all_gather(field, 'gx', axis=0, tiled=True)]
    ppermute x0 -> x11, starting transfers between devices: none -> 41.9 us  [the longest x9 35.9 us: shift(): return lax.ppermute(a, axis, [(i, (i + d) % size) for i in range(size)])]
    all_to_all x0 -> x3, waiting for transfers between devices: none -> 36.2 us  [exchange(): return lax.all_to_all(a, axes, 0, 0)]
    all_to_all x0 -> x1, blocking collectives: none -> 35.1 us  [exchange(): return lax.all_to_all(a, axes, 0, 0)]
    all_to_all x0 -> x3, starting transfers between devices: none -> 23.5 us  [exchange(): return lax.all_to_all(a, axes, 0, 0)]
  transfers between devices with their start and end apart: 6 -> 14, of which waited for: 6 -> 8; matrix products, arithmetic and copies ran while one was open for 2% -> 1% of each run, Pallas kernels for 0% -> 3%
where the time goes in v3:
time: 166 us; the launch traced here: 165 us
  starting transfers between devices  65.4 us (39%)
  waiting for transfers between devices  46.9 us (28%)
  blocking collectives  35.1 us (21%)
  Pallas kernels  8.74 us (5%)
  local copies, waits for them, and re-layouts  4.39 us (3%)
  other arithmetic  4.02 us (2%)
    all_to_all x3, waiting for transfers between devices, exchange(): return lax.all_to_all(a, axes, 0, 0)  36.2 us
    ppermute x9, starting transfers between devices, shift(): return lax.ppermute(a, axis, [(i, (i + d) % size) for i in range(size)])  35.9 us
    all_to_all x1, blocking collectives, exchange(): return lax.all_to_all(a, axes, 0, 0)  35.1 us
    all_to_all x3, starting transfers between devices, exchange(): return lax.all_to_all(a, axes, 0, 0)  23.5 us
    pallas_call x4, Pallas kernels, call(): pl.pallas_call(kernel, out_shape=outs, in_specs=[pl.BlockSpec(memory_spac...  8.74 us
    ppermute x9, waiting for transfers between devices, shift(): return lax.ppermute(a, axis, [(i, (i + d) % size) for i in range(size)])  6.69 us
    ppermute x1, starting transfers between devices, per_device(): z_other = lax.ppermute(z, 'c', [(0, 1), (1, 0)])  3.6 us
  transfers between devices with their start and end apart: 14, of which 8 were waited for; matrix products, arithmetic and copies ran while one was open for 1% of the time, Pallas kernels for 3%

profile of v3, /device:TPU:1, one launch (start us, length us, event | category | flops | bytes accessed | tf_op | source)
XLA Modules:
  0.0 165.5 jit_solution(11341135327619814496)
XLA Ops:
  0.6 0.0 copy-start
  0.7 1.6 copy.18
  2.3 0.0 copy-done
  2.3 1.3 pad_maximum_fusion
  3.6 0.0 copy-start.1
  3.6 7.8 %all-to-all-start = ((f32[8,3,128,128]{3,2,1,0:T(8,128)}), f32[8,3,128,128]{3,2,1,0:T(8,128)S(1)}, u32[]{:S(2)}, u32[]{:S(2)}) async-start(f32[8,3,128,128]{3,2,1,0:T(8,128)} %pad_maximum_fusion), calls=%async_computation | async-start | bytes 3145728 | tf_op jit(solution)/shard_map/all_to_all | solution.py:15
  11.4 0.0 copy-done.1
  11.4 5.8 %collective-permute-start.1 = (f32[128,128]{1,0:T(8,128)S(1)}, f32[128,128]{1,0:T(8,128)S(1)}, u32[]{:S(2)}, u32[]{:S(2)}) collective-permute-start(f32[128,128]{1,0:T(8,128)S(1)} %copy-done.1), channel_id=1, source_target_pairs={{0,32},{16,48},{32,0},{48,16},{1,33},{17,49},{33,1},{49,17},{2,34}... | collective-permute-start | bytes 196616 | tf_op jit(solution)/shard_map/ppermute | solution.py:19
  17.2 4.0 %collective-permute-start = (f32[128,128]{1,0:T(8,128)S(1)}, f32[128,128]{1,0:T(8,128)S(1)}, u32[]{:S(2)}, u32[]{:S(2)}) collective-permute-start(f32[128,128]{1,0:T(8,128)S(1)} %copy-done.1), channel_id=1, source_target_pairs={{0,16},{16,32},{32,48},{48,0},{1,17},{17,33},{33,49},{49,1},{2,18}... | collective-permute-start | bytes 196616 | tf_op jit(solution)/shard_map/ppermute | solution.py:19
  21.2 3.1 %collective-permute-start.2 = (f32[128,128]{1,0:T(8,128)S(1)}, f32[128,128]{1,0:T(8,128)S(1)}, u32[]{:S(2)}, u32[]{:S(2)}) collective-permute-start(f32[128,128]{1,0:T(8,128)S(1)} %copy-done.1), channel_id=1, source_target_pairs={{0,48},{16,0},{32,16},{48,32},{1,49},{17,1},{33,17},{49,33},{2,50}... | collective-permute-start | bytes 196616 | tf_op jit(solution)/shard_map/ppermute | solution.py:19
  24.3 0.0 collective-permute-done.1.v2
  24.3 0.0 collective-permute-done.v1
  24.3 2.5 %collective-permute-done.2.v3 = f32[128,128]{1,0:T(8,128)S(1)} collective-permute-done((f32[128,128]{1,0:T(8,128)S(1)}, f32[128,128]{1,0:T(8,128)S(1)}, u32[]{:S(2)}, u32[]{:S(2)}) %collective-permute-start.2) | collective-permute-done | bytes 65568 | tf_op jit(solution)/shard_map/ppermute | solution.py:19
  26.8 25.0 %all-to-all-done.own = f32[8,3,128,128]{3,2,1,0:T(8,128)S(1)} async-done(((f32[8,3,128,128]{3,2,1,0:T(8,128)}), f32[8,3,128,128]{3,2,1,0:T(8,128)S(1)}, u32[]{:S(2)}, u32[]{:S(2)}) %all-to-all-start) | async-done | bytes 1572896 | tf_op jit(solution)/shard_map/all_to_all | solution.py:15
  51.8 2.4 %collective-permute-start.3 = (f32[8,3,128,128]{3,2,1,0:T(8,128)S(1)}, f32[8,3,128,128]{3,2,1,0:T(8,128)S(1)}, u32[]{:S(2)}, u32[]{:S(2)}) collective-permute-start(f32[8,3,128,128]{3,2,1,0:T(8,128)S(1)} %all-to-all-done.own), channel_id=1, source_target_pairs={{0,1},{1,0},{2,3},{3,2},{4,5},{5,4},{6,7},{7,6},{8,9},{9,8},{10,11... | collective-permute-start | bytes 4718600 | tf_op jit(solution)/shard_map/ppermute | solution.py:147
  54.2 0.1 pad_add_fusion.ids
  54.3 2.9 %collective-permute-done.3.other = f32[8,3,128,128]{3,2,1,0:T(8,128)S(1)} collective-permute-done((f32[8,3,128,128]{3,2,1,0:T(8,128)S(1)}, f32[8,3,128,128]{3,2,1,0:T(8,128)S(1)}, u32[]{:S(2)}, u32[]{:S(2)}) %collective-permute-start.3) | collective-permute-done | bytes 1572896 | tf_op jit(solution)/shard_map/ppermute | solution.py:147
  57.2 4.4 %shard_map.58.after = f32[4,64,16,128]{3,2,1,0:T(8,128)} custom-call(s32[3]{0:T(128)S(1)} %pad_add_fusion.ids, f32[8,3,128,128]{3,2,1,0:T(8,128)S(1)} %all-to-all-done.own, f32[8,3,128,128]{3,2,1,0:T(8,128)S(1)} %collective-permute-done.3.other), custom_call_target="tpu_custom_call" | custom-call | flops 1610612736 | bytes 4194304 | tf_op jit(solution)/shard_map/pallas_call | solution.py:123
  61.7 4.5 %all-to-all-start.1 = ((f32[4,64,16,128]{3,2,1,0:T(8,128)}), f32[4,64,16,128]{3,2,1,0:T(8,128)}, u32[]{:S(2)}, u32[]{:S(2)}) async-start(f32[4,64,16,128]{3,2,1,0:T(8,128)} %shard_map.58.after), calls=%async_computation.1 | async-start | bytes 4194304 | tf_op jit(solution)/shard_map/all_to_all | solution.py:15
  66.1 1.6 shard_map.59
  67.7 4.0 %collective-permute-start.4 = (f32[128,128]{1,0:T(8,128)S(1)}, f32[128,128]{1,0:T(8,128)S(1)}, u32[]{:S(2)}, u32[]{:S(2)}) collective-permute-start(f32[128,128]{1,0:T(8,128)S(1)} %get-tuple-element.18), channel_id=1, source_target_pairs={{0,16},{16,32},{32,48},{48,0},{1,17},{17,33},{33,49},{49,1},{2,18}... | collective-permute-start | bytes 196616 | tf_op jit(solution)/shard_map/ppermute | solution.py:19
  71.7 5.8 %collective-permute-start.5 = (f32[128,128]{1,0:T(8,128)S(1)}, f32[128,128]{1,0:T(8,128)S(1)}, u32[]{:S(2)}, u32[]{:S(2)}) collective-permute-start(f32[128,128]{1,0:T(8,128)S(1)} %get-tuple-element.19), channel_id=1, source_target_pairs={{0,32},{16,48},{32,0},{48,16},{1,33},{17,49},{33,1},{49,17},{2,34}... | collective-permute-start | bytes 196616 | tf_op jit(solution)/shard_map/ppermute | solution.py:19
  77.5 2.2 %collective-permute-start.6 = (f32[128,128]{1,0:T(8,128)S(1)}, f32[128,128]{1,0:T(8,128)S(1)}, u32[]{:S(2)}, u32[]{:S(2)}) collective-permute-start(f32[128,128]{1,0:T(8,128)S(1)} %get-tuple-element.20), channel_id=1, source_target_pairs={{0,48},{16,0},{32,16},{48,32},{1,49},{17,1},{33,17},{49,33},{2,50}... | collective-permute-start | bytes 196616 | tf_op jit(solution)/shard_map/ppermute | solution.py:19
  79.7 0.0 collective-permute-done.4
  79.7 1.6 collective-permute-done.5
  81.3 1.6 collective-permute-done.6
  83.0 3.6 %collective-permute-start.7 = (f32[4,128,128]{2,1,0:T(8,128)S(1)}, f32[4,128,128]{2,1,0:T(8,128)S(1)}, u32[]{:S(2)}, u32[]{:S(2)}) collective-permute-start(f32[4,128,128]{2,1,0:T(8,128)S(1)} %pad_maximum_fusion.2.own.z), channel_id=1, source_target_pairs={{0,1},{1,0},{2,3},{3,2},{4,5},{5,4},{6,7},{7,6},{8,9},{9,8},{10,11... | collective-permute-start | bytes 786440 | tf_op jit(solution)/shard_map/ppermute | solution.py:173
  86.6 1.1 collective-permute-done.7.other
  87.7 1.1 shard_map.60
  88.8 3.6 %collective-permute-start.8 = (f32[32,8,128]{2,1,0:T(8,128)S(1)}, f32[32,8,128]{2,1,0:T(8,128)S(1)}, u32[]{:S(2)}, u32[]{:S(2)}) collective-permute-start(f32[32,8,128]{2,1,0:T(8,128)S(1)} %get-tuple-element.22), channel_id=1, source_target_pairs={{0,2},{2,4},{4,6},{6,0},{1,3},{3,5},{5,7},{7,1},{8,10},{10,12},{12... | collective-permute-start | bytes 393224 | tf_op jit(solution)/shard_map/ppermute | solution.py:19
  92.4 4.3 %collective-permute-start.9 = (f32[32,8,128]{2,1,0:T(8,128)S(1)}, f32[32,8,128]{2,1,0:T(8,128)S(1)}, u32[]{:S(2)}, u32[]{:S(2)}) collective-permute-start(f32[32,8,128]{2,1,0:T(8,128)S(1)} %get-tuple-element.23), channel_id=1, source_target_pairs={{0,4},{2,6},{4,0},{6,2},{1,5},{3,7},{5,1},{7,3},{8,12},{10,14},{12... | collective-permute-start | bytes 393224 | tf_op jit(solution)/shard_map/ppermute | solution.py:19
  96.7 3.1 %collective-permute-start.10 = (f32[32,8,128]{2,1,0:T(8,128)S(1)}, f32[32,8,128]{2,1,0:T(8,128)S(1)}, u32[]{:S(2)}, u32[]{:S(2)}) collective-permute-start(f32[32,8,128]{2,1,0:T(8,128)S(1)} %get-tuple-element.24), channel_id=1, source_target_pairs={{0,6},{2,0},{4,2},{6,4},{1,7},{3,1},{5,3},{7,5},{8,14},{10,8},{12,... | collective-permute-start | bytes 393224 | tf_op jit(solution)/shard_map/ppermute | solution.py:19
  99.8 1.6 shard_map.61
  101.5 0.0 collective-permute-done.8
  101.5 0.0 collective-permute-done.9
  101.5 0.9 collective-permute-done.10
  102.5 0.0 all-to-all-done.1
  102.5 1.8 %reduce_sum.27 = f32[64,16,128]{2,1,0:T(8,128)S(1)} reduce(f32[4,64,16,128]{3,2,1,0:T(8,128)} %all-to-all-done.1, f32[]{:T(128)} %constant.30.clone.1), dimensions={0}, to_apply=%region_0.0 | reduce | flops 393216 | bytes 2621444 | tf_op jit(solution)/shard_map/reduce_sum | solution.py:186
  104.3 0.1 pad_maximum_fusion.1
  104.4 35.1 %all_to_all.20 = f32[64,32,128]{2,1,0:T(8,128)S(1)} all-to-all(f32[64,32,128]{2,1,0:T(8,128)S(1)} %pad_maximum_fusion.1), channel_id=1, replica_groups=mesh['yh'=2,'yl'=4,'zl'=4,'zh'=2,'x'=4,'c'=2] {'yh','yl','zl','zh'}, dimensions={0} | all-to-all | bytes 2097152 | tf_op jit(solution)/shard_map/all_to_all | solution.py:15
  139.5 0.1 slice_reduce_fusion.1
  139.6 0.7 broadcast_in_dim.15
  140.3 11.3 %all-to-all-start.3 = ((f32[64,8,128]{2,1,0:T(8,128)}), f32[64,8,128]{2,1,0:T(8,128)S(1)}, u32[]{:S(2)}, u32[]{:S(2)}) async-start(f32[64,8,128]{2,1,0:T(8,128)} %broadcast_in_dim.15), calls=%async_computation.3 | async-start | bytes 524288 | tf_op jit(solution)/shard_map/all_to_all | solution.py:15
  151.6 0.2 reshape.34
  151.9 0.1 copy.15
  152.0 0.8 copy.16
  152.8 0.1 slice_reduce_fusion
  152.9 0.6 multiply_bitcast_fusion
  153.5 11.2 %all-to-all-done.3 = f32[64,8,128]{2,1,0:T(8,128)S(1)} async-done(((f32[64,8,128]{2,1,0:T(8,128)}), f32[64,8,128]{2,1,0:T(8,128)S(1)}, u32[]{:S(2)}, u32[]{:S(2)}) %all-to-all-start.3) | async-done | bytes 262176 | tf_op jit(solution)/shard_map/all_to_all | solution.py:15
  164.7 0.7 copy.13
  (10 shorter events, 0.2 us)
Async XLA Ops:
  0.6 1.6 copy-start
  3.6 7.8 %copy-start.1 = (f32[128,128]{1,0:T(8,128)S(1)}, f32[128,128]{1,0:T(8,128)}, u32[]{:S(2)}) copy-start(f32[128,128]{1,0:T(8,128)} %v0) | copy-start | bytes 196612
  3.6 48.2 %all-to-all-start = ((f32[8,3,128,128]{3,2,1,0:T(8,128)}), f32[8,3,128,128]{3,2,1,0:T(8,128)S(1)}, u32[]{:S(2)}, u32[]{:S(2)}) async-start(f32[8,3,128,128]{3,2,1,0:T(8,128)} %pad_maximum_fusion), calls=%async_computation | async-start | bytes 3145728 | tf_op jit(solution)/shard_map/all_to_all | solution.py:15
  11.4 12.9 %collective-permute-start.1 = (f32[128,128]{1,0:T(8,128)S(1)}, f32[128,128]{1,0:T(8,128)S(1)}, u32[]{:S(2)}, u32[]{:S(2)}) collective-permute-start(f32[128,128]{1,0:T(8,128)S(1)} %copy-done.1), channel_id=1, source_target_pairs={{0,32},{16,48},{32,0},{48,16},{1,33},{17,49},{33,1},{49,17},{2,34}... | collective-permute-start | bytes 196616 | tf_op jit(solution)/shard_map/ppermute | solution.py:19
  17.2 7.1 %collective-permute-start = (f32[128,128]{1,0:T(8,128)S(1)}, f32[128,128]{1,0:T(8,128)S(1)}, u32[]{:S(2)}, u32[]{:S(2)}) collective-permute-start(f32[128,128]{1,0:T(8,128)S(1)} %copy-done.1), channel_id=1, source_target_pairs={{0,16},{16,32},{32,48},{48,0},{1,17},{17,33},{33,49},{49,1},{2,18}... | collective-permute-start | bytes 196616 | tf_op jit(solution)/shard_map/ppermute | solution.py:19
  21.2 5.6 %collective-permute-start.2 = (f32[128,128]{1,0:T(8,128)S(1)}, f32[128,128]{1,0:T(8,128)S(1)}, u32[]{:S(2)}, u32[]{:S(2)}) collective-permute-start(f32[128,128]{1,0:T(8,128)S(1)} %copy-done.1), channel_id=1, source_target_pairs={{0,48},{16,0},{32,16},{48,32},{1,49},{17,1},{33,17},{49,33},{2,50}... | collective-permute-start | bytes 196616 | tf_op jit(solution)/shard_map/ppermute | solution.py:19
  51.8 5.4 %collective-permute-start.3 = (f32[8,3,128,128]{3,2,1,0:T(8,128)S(1)}, f32[8,3,128,128]{3,2,1,0:T(8,128)S(1)}, u32[]{:S(2)}, u32[]{:S(2)}) collective-permute-start(f32[8,3,128,128]{3,2,1,0:T(8,128)S(1)} %all-to-all-done.own), channel_id=1, source_target_pairs={{0,1},{1,0},{2,3},{3,2},{4,5},{5,4},{6,7},{7,6},{8,9},{9,8},{10,11... | collective-permute-start | bytes 4718600 | tf_op jit(solution)/shard_map/ppermute | solution.py:147
  61.7 40.8 %all-to-all-start.1 = ((f32[4,64,16,128]{3,2,1,0:T(8,128)}), f32[4,64,16,128]{3,2,1,0:T(8,128)}, u32[]{:S(2)}, u32[]{:S(2)}) async-start(f32[4,64,16,128]{3,2,1,0:T(8,128)} %shard_map.58.after), calls=%async_computation.1 | async-start | bytes 4194304 | tf_op jit(solution)/shard_map/all_to_all | solution.py:15
  67.7 12.0 %collective-permute-start.4 = (f32[128,128]{1,0:T(8,128)S(1)}, f32[128,128]{1,0:T(8,128)S(1)}, u32[]{:S(2)}, u32[]{:S(2)}) collective-permute-start(f32[128,128]{1,0:T(8,128)S(1)} %get-tuple-element.18), channel_id=1, source_target_pairs={{0,16},{16,32},{32,48},{48,0},{1,17},{17,33},{33,49},{49,1},{2,18}... | collective-permute-start | bytes 196616 | tf_op jit(solution)/shard_map/ppermute | solution.py:19
  71.7 9.6 %collective-permute-start.5 = (f32[128,128]{1,0:T(8,128)S(1)}, f32[128,128]{1,0:T(8,128)S(1)}, u32[]{:S(2)}, u32[]{:S(2)}) collective-permute-start(f32[128,128]{1,0:T(8,128)S(1)} %get-tuple-element.19), channel_id=1, source_target_pairs={{0,32},{16,48},{32,0},{48,16},{1,33},{17,49},{33,1},{49,17},{2,34}... | collective-permute-start | bytes 196616 | tf_op jit(solution)/shard_map/ppermute | solution.py:19
  77.5 5.4 %collective-permute-start.6 = (f32[128,128]{1,0:T(8,128)S(1)}, f32[128,128]{1,0:T(8,128)S(1)}, u32[]{:S(2)}, u32[]{:S(2)}) collective-permute-start(f32[128,128]{1,0:T(8,128)S(1)} %get-tuple-element.20), channel_id=1, source_target_pairs={{0,48},{16,0},{32,16},{48,32},{1,49},{17,1},{33,17},{49,33},{2,50}... | collective-permute-start | bytes 196616 | tf_op jit(solution)/shard_map/ppermute | solution.py:19
  83.0 4.7 %collective-permute-start.7 = (f32[4,128,128]{2,1,0:T(8,128)S(1)}, f32[4,128,128]{2,1,0:T(8,128)S(1)}, u32[]{:S(2)}, u32[]{:S(2)}) collective-permute-start(f32[4,128,128]{2,1,0:T(8,128)S(1)} %pad_maximum_fusion.2.own.z), channel_id=1, source_target_pairs={{0,1},{1,0},{2,3},{3,2},{4,5},{5,4},{6,7},{7,6},{8,9},{9,8},{10,11... | collective-permute-start | bytes 786440 | tf_op jit(solution)/shard_map/ppermute | solution.py:173
  88.8 12.7 %collective-permute-start.8 = (f32[32,8,128]{2,1,0:T(8,128)S(1)}, f32[32,8,128]{2,1,0:T(8,128)S(1)}, u32[]{:S(2)}, u32[]{:S(2)}) collective-permute-start(f32[32,8,128]{2,1,0:T(8,128)S(1)} %get-tuple-element.22), channel_id=1, source_target_pairs={{0,2},{2,4},{4,6},{6,0},{1,3},{3,5},{5,7},{7,1},{8,10},{10,12},{12... | collective-permute-start | bytes 393224 | tf_op jit(solution)/shard_map/ppermute | solution.py:19
  92.4 9.1 %collective-permute-start.9 = (f32[32,8,128]{2,1,0:T(8,128)S(1)}, f32[32,8,128]{2,1,0:T(8,128)S(1)}, u32[]{:S(2)}, u32[]{:S(2)}) collective-permute-start(f32[32,8,128]{2,1,0:T(8,128)S(1)} %get-tuple-element.23), channel_id=1, source_target_pairs={{0,4},{2,6},{4,0},{6,2},{1,5},{3,7},{5,1},{7,3},{8,12},{10,14},{12... | collective-permute-start | bytes 393224 | tf_op jit(solution)/shard_map/ppermute | solution.py:19
  96.7 5.7 %collective-permute-start.10 = (f32[32,8,128]{2,1,0:T(8,128)S(1)}, f32[32,8,128]{2,1,0:T(8,128)S(1)}, u32[]{:S(2)}, u32[]{:S(2)}) collective-permute-start(f32[32,8,128]{2,1,0:T(8,128)S(1)} %get-tuple-element.24), channel_id=1, source_target_pairs={{0,6},{2,0},{4,2},{6,4},{1,7},{3,1},{5,3},{7,5},{8,14},{10,8},{12,... | collective-permute-start | bytes 393224 | tf_op jit(solution)/shard_map/ppermute | solution.py:19
  140.3 24.4 %all-to-all-start.3 = ((f32[64,8,128]{2,1,0:T(8,128)}), f32[64,8,128]{2,1,0:T(8,128)S(1)}, u32[]{:S(2)}, u32[]{:S(2)}) async-start(f32[64,8,128]{2,1,0:T(8,128)} %broadcast_in_dim.15), calls=%async_computation.3 | async-start | bytes 524288 | tf_op jit(solution)/shard_map/all_to_all | solution.py:15

commit v4 on v3

--- a/solution.py
+++ b/solution.py
@@ -31,7 +31,7 @@
     return one(a[0], b[0]) + (one(a[0], b[1]) + one(a[1], b[0]))
 
 
-def project_kernel(ids, own, other, after, o0, o1, o2, o3, res):
+def project_kernel(ids, own, other, o0, o1, o2, o3, res):
     c = ids[1]
     total = [jnp.zeros((128, 256), F32)] * 2
     for y in range(NY):
@@ -54,31 +54,27 @@
 
 
 def gram_one_kernel(ids, own, other, out, hi, lo, row_hi, row_lo):
-    n = pl.program_id(0)
-
-    @pl.when(n == 0)
-    def _():
-        for i, ref in enumerate((own, other)):
-            for k in range(2):
-                for y in range(NY):
-                    col = 256 * i + 128 * k
-                    a, b = split(ref[y, k])
-                    hi[128 * y : 128 * y + 128, col : col + 128] = a
-                    lo[128 * y : 128 * y + 128, col : col + 128] = b
+    for i, ref in enumerate((own, other)):
+        for k in range(2):
+            for y in range(NY):
+                col = 256 * i + 128 * k
+                a, b = split(ref[y, k])
+                hi[128 * y : 128 * y + 128, col : col + 128] = a
+                lo[128 * y : 128 * y + 128, col : col + 128] = b
+    for x in range(NX):
+        for b in range(8):
+            src = pl.ds(pl.multiple_of(128 * b + 32 * x + 16 * ids[1], 16), 16)
+            dst = slice(128 * x + 16 * b, 128 * x + 16 * b + 16)
+            row_hi[dst, :] = hi[src, :]
+            row_lo[dst, :] = lo[src, :]
+    for n in range(4):
+        cols = slice(256 * n, 256 * n + 256)
+        r = dot3((row_hi[...], row_lo[...]), (hi[cols, :], lo[cols, :]), ((1,), (1,)))
         for x in range(NX):
-            for b in range(8):
-                src = pl.ds(pl.multiple_of(128 * b + 32 * x + 16 * ids[1], 16), 16)
-                dst = slice(128 * x + 16 * b, 128 * x + 16 * b + 16)
-                row_hi[dst, :] = hi[src, :]
-                row_lo[dst, :] = lo[src, :]
-
-    cols = pl.ds(pl.multiple_of(256 * n, 256), 256)
-    r = dot3((row_hi[...], row_lo[...]), (hi[cols, :], lo[cols, :]), ((1,), (1,)))
-    for x in range(NX):
-        for y in range(2):
-            for b in range(8):
-                at = 128 * x + 16 * b
-                out[x, 8 * y + b] = r[at : at + 16, 128 * y : 128 * y + 128]
+            for y in range(2):
+                for b in range(8):
+                    at = 128 * x + 16 * b
+                    out[x, 16 * n + 8 * y + b] = r[at : at + 16, 128 * y : 128 * y + 128]
 
 
 def gram_two_kernel(ids, own, other, o0, o1, o2, o3, hi, lo, res):
@@ -116,20 +112,18 @@
             out[y, zl] = jnp.concatenate([part, part], axis=0)
 
 
-def call(kernel, out_shape, flops, *args, scratch=(), grid=None, out_specs=None, unread=0):
+def call(kernel, out_shape, flops, *args, scratch=(), unread=0):
     vmem = pl.BlockSpec(memory_space=pltpu.VMEM)
     outs = jax.tree.map(lambda s: jax.ShapeDtypeStruct(s, F32), out_shape, is_leaf=lambda s: isinstance(s[0], int))
-    kw = {} if grid is None else {"grid": grid}
     return pl.pallas_call(
         kernel,
         out_shape=outs,
         in_specs=[pl.BlockSpec(memory_space=pltpu.SMEM)] + [vmem] * (len(args) - 1 - unread)
         + [pl.BlockSpec(memory_space=pl.ANY)] * unread,
-        out_specs=jax.tree.map(lambda _: vmem, outs) if out_specs is None else out_specs,
+        out_specs=jax.tree.map(lambda _: vmem, outs),
         scratch_shapes=list(scratch),
         compiler_params=pltpu.CompilerParams(vmem_limit_bytes=32 * 2**20),
         cost_estimate=pl.CostEstimate(flops=flops, bytes_accessed=4 * 2**20, transcendentals=0),
-        **kw,
     )(*args)
 
 
@@ -153,8 +147,6 @@
         ids,
         own,
         other,
-        grid=(4,),
-        out_specs=pl.BlockSpec((NX, 16, 16, 128), lambda n: (0, n, 0, 0)),
         scratch=[pltpu.VMEM((1024, 512), BF16)] * 2 + [pltpu.VMEM((512, 512), BF16)] * 2,
     )
     z = call(
@@ -164,8 +156,6 @@
         ids,
         own,
         other,
-        g1,
-        unread=1,
         scratch=[pltpu.VMEM((NZL, 128, 128), F32)],
     )
     z = jnp.stack([z[0]] + [shift(z[d], "zl", NZL, d) for d in range(1, NZL)])

time: 166 us -> 166 us (level)
  Pallas kernels: 8.74 us -> 6.94 us
    pallas_call x4, Pallas kernels: 8.74 us -> 6.94 us  [call(): pl.pallas_call(kernel, out_shape=outs, in_specs=[pl.BlockSpec(memory_spac...]
    unnamed x6 -> x8, local copies, waits for them, and re-layouts: 2.45 us -> 3.75 us
where the time goes in v4:
time: 166 us; the launch traced here: 165 us
  starting transfers between devices  65.4 us (39%)
  waiting for transfers between devices  46.9 us (28%)
  blocking collectives  35.1 us (21%)
  Pallas kernels  6.94 us (4%)
  local copies, waits for them, and re-layouts  5.69 us (3%)
  other arithmetic  4.01 us (2%)
    all_to_all x3, waiting for transfers between devices, exchange(): return lax.all_to_all(a, axes, 0, 0)  36.2 us
    ppermute x9, starting transfers between devices, shift(): return lax.ppermute(a, axis, [(i, (i + d) % size) for i in range(size)])  35.9 us
    all_to_all x1, blocking collectives, exchange(): return lax.all_to_all(a, axes, 0, 0)  35.1 us
    all_to_all x3, starting transfers between devices, exchange(): return lax.all_to_all(a, axes, 0, 0)  23.5 us
    pallas_call x4, Pallas kernels, call(): pl.pallas_call(kernel, out_shape=outs, in_specs=[pl.BlockSpec(memory_spac...  6.94 us
    ppermute x9, waiting for transfers between devices, shift(): return lax.ppermute(a, axis, [(i, (i + d) % size) for i in range(size)])  6.69 us
    unnamed x8, local copies, waits for them, and re-layouts  3.75 us
    ppermute x1, starting transfers between devices, per_device(): z_other = lax.ppermute(z, 'c', [(0, 1), (1, 0)])  3.59 us
  transfers between devices with their start and end apart: 14, of which 8 were waited for; matrix products, arithmetic and copies ran while one was open for 1% of the time, Pallas kernels for 3%

profile of v4, /device:TPU:1, one launch (start us, length us, event | category | flops | bytes accessed | tf_op | source)
XLA Modules:
  0.0 165.0 jit_solution(10006451363336241492)
XLA Ops:
  0.6 0.0 copy-start
  0.7 1.6 copy.18
  2.3 0.0 copy-done
  2.3 1.3 pad_maximum_fusion
  3.6 0.0 copy-start.2
  3.6 7.8 %all-to-all-start = ((f32[8,3,128,128]{3,2,1,0:T(8,128)}), f32[8,3,128,128]{3,2,1,0:T(8,128)S(1)}, u32[]{:S(2)}, u32[]{:S(2)}) async-start(f32[8,3,128,128]{3,2,1,0:T(8,128)} %pad_maximum_fusion), calls=%async_computation | async-start | bytes 3145728 | tf_op jit(solution)/shard_map/all_to_all | solution.py:15
  11.4 0.0 copy-done.2
  11.4 5.8 %collective-permute-start.1 = (f32[128,128]{1,0:T(8,128)S(1)}, f32[128,128]{1,0:T(8,128)S(1)}, u32[]{:S(2)}, u32[]{:S(2)}) collective-permute-start(f32[128,128]{1,0:T(8,128)S(1)} %copy-done.2), channel_id=1, source_target_pairs={{0,32},{16,48},{32,0},{48,16},{1,33},{17,49},{33,1},{49,17},{2,34}... | collective-permute-start | bytes 196616 | tf_op jit(solution)/shard_map/ppermute | solution.py:19
  17.2 4.0 %collective-permute-start = (f32[128,128]{1,0:T(8,128)S(1)}, f32[128,128]{1,0:T(8,128)S(1)}, u32[]{:S(2)}, u32[]{:S(2)}) collective-permute-start(f32[128,128]{1,0:T(8,128)S(1)} %copy-done.2), channel_id=1, source_target_pairs={{0,16},{16,32},{32,48},{48,0},{1,17},{17,33},{33,49},{49,1},{2,18}... | collective-permute-start | bytes 196616 | tf_op jit(solution)/shard_map/ppermute | solution.py:19
  21.2 3.1 %collective-permute-start.2 = (f32[128,128]{1,0:T(8,128)S(1)}, f32[128,128]{1,0:T(8,128)S(1)}, u32[]{:S(2)}, u32[]{:S(2)}) collective-permute-start(f32[128,128]{1,0:T(8,128)S(1)} %copy-done.2), channel_id=1, source_target_pairs={{0,48},{16,0},{32,16},{48,32},{1,49},{17,1},{33,17},{49,33},{2,50}... | collective-permute-start | bytes 196616 | tf_op jit(solution)/shard_map/ppermute | solution.py:19
  24.3 0.0 collective-permute-done.1.v2
  24.3 0.0 collective-permute-done.v1
  24.3 2.5 %collective-permute-done.2.v3 = f32[128,128]{1,0:T(8,128)S(1)} collective-permute-done((f32[128,128]{1,0:T(8,128)S(1)}, f32[128,128]{1,0:T(8,128)S(1)}, u32[]{:S(2)}, u32[]{:S(2)}) %collective-permute-start.2) | collective-permute-done | bytes 65568 | tf_op jit(solution)/shard_map/ppermute | solution.py:19
  26.8 25.0 %all-to-all-done.own = f32[8,3,128,128]{3,2,1,0:T(8,128)S(1)} async-done(((f32[8,3,128,128]{3,2,1,0:T(8,128)}), f32[8,3,128,128]{3,2,1,0:T(8,128)S(1)}, u32[]{:S(2)}, u32[]{:S(2)}) %all-to-all-start) | async-done | bytes 1572896 | tf_op jit(solution)/shard_map/all_to_all | solution.py:15
  51.8 2.4 %collective-permute-start.3 = (f32[8,3,128,128]{3,2,1,0:T(8,128)S(1)}, f32[8,3,128,128]{3,2,1,0:T(8,128)S(1)}, u32[]{:S(2)}, u32[]{:S(2)}) collective-permute-start(f32[8,3,128,128]{3,2,1,0:T(8,128)S(1)} %all-to-all-done.own), channel_id=1, source_target_pairs={{0,1},{1,0},{2,3},{3,2},{4,5},{5,4},{6,7},{7,6},{8,9},{9,8},{10,11... | collective-permute-start | bytes 4718600 | tf_op jit(solution)/shard_map/ppermute | solution.py:141
  54.2 0.1 pad_add_fusion.ids
  54.3 2.9 %collective-permute-done.3.other = f32[8,3,128,128]{3,2,1,0:T(8,128)S(1)} collective-permute-done((f32[8,3,128,128]{3,2,1,0:T(8,128)S(1)}, f32[8,3,128,128]{3,2,1,0:T(8,128)S(1)}, u32[]{:S(2)}, u32[]{:S(2)}) %collective-permute-start.3) | collective-permute-done | bytes 1572896 | tf_op jit(solution)/shard_map/ppermute | solution.py:141
  57.2 2.6 %shard_map.58 = f32[4,64,16,128]{3,2,1,0:T(8,128)S(1)} custom-call(s32[3]{0:T(128)S(1)} %pad_add_fusion.ids, f32[8,3,128,128]{3,2,1,0:T(8,128)S(1)} %all-to-all-done.own, f32[8,3,128,128]{3,2,1,0:T(8,128)S(1)} %collective-permute-done.3.other), custom_call_target="tpu_custom_call" | custom-call | flops 1610612736 | bytes 4194304 | tf_op jit(solution)/shard_map/pallas_call | solution.py:118
  59.9 0.0 copy-start.1
  59.9 1.3 copy-done.1
  61.2 4.4 %all-to-all-start.1 = ((f32[4,64,16,128]{3,2,1,0:T(8,128)}), f32[4,64,16,128]{3,2,1,0:T(8,128)}, u32[]{:S(2)}, u32[]{:S(2)}) async-start(f32[4,64,16,128]{3,2,1,0:T(8,128)} %copy-done.1), calls=%async_computation.1 | async-start | bytes 4194304 | tf_op jit(solution)/shard_map/all_to_all | solution.py:15
  65.6 1.6 shard_map.59
  67.2 4.0 %collective-permute-start.4 = (f32[128,128]{1,0:T(8,128)S(1)}, f32[128,128]{1,0:T(8,128)S(1)}, u32[]{:S(2)}, u32[]{:S(2)}) collective-permute-start(f32[128,128]{1,0:T(8,128)S(1)} %get-tuple-element.18), channel_id=1, source_target_pairs={{0,16},{16,32},{32,48},{48,0},{1,17},{17,33},{33,49},{49,1},{2,18}... | collective-permute-start | bytes 196616 | tf_op jit(solution)/shard_map/ppermute | solution.py:19
  71.2 5.8 %collective-permute-start.5 = (f32[128,128]{1,0:T(8,128)S(1)}, f32[128,128]{1,0:T(8,128)S(1)}, u32[]{:S(2)}, u32[]{:S(2)}) collective-permute-start(f32[128,128]{1,0:T(8,128)S(1)} %get-tuple-element.19), channel_id=1, source_target_pairs={{0,32},{16,48},{32,0},{48,16},{1,33},{17,49},{33,1},{49,17},{2,34}... | collective-permute-start | bytes 196616 | tf_op jit(solution)/shard_map/ppermute | solution.py:19
  77.0 2.2 %collective-permute-start.6 = (f32[128,128]{1,0:T(8,128)S(1)}, f32[128,128]{1,0:T(8,128)S(1)}, u32[]{:S(2)}, u32[]{:S(2)}) collective-permute-start(f32[128,128]{1,0:T(8,128)S(1)} %get-tuple-element.20), channel_id=1, source_target_pairs={{0,48},{16,0},{32,16},{48,32},{1,49},{17,1},{33,17},{49,33},{2,50}... | collective-permute-start | bytes 196616 | tf_op jit(solution)/shard_map/ppermute | solution.py:19
  79.2 0.0 collective-permute-done.4
  79.2 1.6 collective-permute-done.5
  80.9 1.6 collective-permute-done.6
  82.5 3.6 %collective-permute-start.7 = (f32[4,128,128]{2,1,0:T(8,128)S(1)}, f32[4,128,128]{2,1,0:T(8,128)S(1)}, u32[]{:S(2)}, u32[]{:S(2)}) collective-permute-start(f32[4,128,128]{2,1,0:T(8,128)S(1)} %pad_maximum_fusion.2.own.z), channel_id=1, source_target_pairs={{0,1},{1,0},{2,3},{3,2},{4,5},{5,4},{6,7},{7,6},{8,9},{9,8},{10,11... | collective-permute-start | bytes 786440 | tf_op jit(solution)/shard_map/ppermute | solution.py:163
  86.1 1.1 collective-permute-done.7.other
  87.2 1.1 shard_map.60
  88.3 3.6 %collective-permute-start.8 = (f32[32,8,128]{2,1,0:T(8,128)S(1)}, f32[32,8,128]{2,1,0:T(8,128)S(1)}, u32[]{:S(2)}, u32[]{:S(2)}) collective-permute-start(f32[32,8,128]{2,1,0:T(8,128)S(1)} %get-tuple-element.22), channel_id=1, source_target_pairs={{0,2},{2,4},{4,6},{6,0},{1,3},{3,5},{5,7},{7,1},{8,10},{10,12},{12... | collective-permute-start | bytes 393224 | tf_op jit(solution)/shard_map/ppermute | solution.py:19
  91.9 4.3 %collective-permute-start.9 = (f32[32,8,128]{2,1,0:T(8,128)S(1)}, f32[32,8,128]{2,1,0:T(8,128)S(1)}, u32[]{:S(2)}, u32[]{:S(2)}) collective-permute-start(f32[32,8,128]{2,1,0:T(8,128)S(1)} %get-tuple-element.23), channel_id=1, source_target_pairs={{0,4},{2,6},{4,0},{6,2},{1,5},{3,7},{5,1},{7,3},{8,12},{10,14},{12... | collective-permute-start | bytes 393224 | tf_op jit(solution)/shard_map/ppermute | solution.py:19
  96.2 3.1 %collective-permute-start.10 = (f32[32,8,128]{2,1,0:T(8,128)S(1)}, f32[32,8,128]{2,1,0:T(8,128)S(1)}, u32[]{:S(2)}, u32[]{:S(2)}) collective-permute-start(f32[32,8,128]{2,1,0:T(8,128)S(1)} %get-tuple-element.24), channel_id=1, source_target_pairs={{0,6},{2,0},{4,2},{6,4},{1,7},{3,1},{5,3},{7,5},{8,14},{10,8},{12,... | collective-permute-start | bytes 393224 | tf_op jit(solution)/shard_map/ppermute | solution.py:19
  99.3 1.6 shard_map.61
  101.0 0.0 collective-permute-done.8
  101.0 0.0 collective-permute-done.9
  101.0 0.9 collective-permute-done.10
  102.0 0.0 all-to-all-done.1
  102.0 1.8 %reduce_sum.27 = f32[64,16,128]{2,1,0:T(8,128)S(1)} reduce(f32[4,64,16,128]{3,2,1,0:T(8,128)} %all-to-all-done.1, f32[]{:T(128)} %constant.30.clone.1), dimensions={0}, to_apply=%region_0.0 | reduce | flops 393216 | bytes 2621444 | tf_op jit(solution)/shard_map/reduce_sum | solution.py:176
  103.8 0.1 pad_maximum_fusion.1
  103.9 35.1 %all_to_all.20 = f32[64,32,128]{2,1,0:T(8,128)S(1)} all-to-all(f32[64,32,128]{2,1,0:T(8,128)S(1)} %pad_maximum_fusion.1), channel_id=1, replica_groups=mesh['yh'=2,'yl'=4,'zl'=4,'zh'=2,'x'=4,'c'=2] {'yh','yl','zl','zh'}, dimensions={0} | all-to-all | bytes 2097152 | tf_op jit(solution)/shard_map/all_to_all | solution.py:15
  139.0 0.1 slice_reduce_fusion.1
  139.0 0.7 broadcast_in_dim.15
  139.8 11.3 %all-to-all-start.3 = ((f32[64,8,128]{2,1,0:T(8,128)}), f32[64,8,128]{2,1,0:T(8,128)S(1)}, u32[]{:S(2)}, u32[]{:S(2)}) async-start(f32[64,8,128]{2,1,0:T(8,128)} %broadcast_in_dim.15), calls=%async_computation.3 | async-start | bytes 524288 | tf_op jit(solution)/shard_map/all_to_all | solution.py:15
  151.1 0.2 reshape.34
  151.4 0.1 copy.15
  151.5 0.8 copy.16
  152.3 0.1 slice_reduce_fusion
  152.4 0.6 multiply_bitcast_fusion
  153.0 11.2 %all-to-all-done.3 = f32[64,8,128]{2,1,0:T(8,128)S(1)} async-done(((f32[64,8,128]{2,1,0:T(8,128)}), f32[64,8,128]{2,1,0:T(8,128)S(1)}, u32[]{:S(2)}, u32[]{:S(2)}) %all-to-all-start.3) | async-done | bytes 262176 | tf_op jit(solution)/shard_map/all_to_all | solution.py:15
  164.2 0.7 copy.13
  (10 shorter events, 0.2 us)
Async XLA Ops:
  0.6 1.6 copy-start
  3.6 7.8 %copy-start.2 = (f32[128,128]{1,0:T(8,128)S(1)}, f32[128,128]{1,0:T(8,128)}, u32[]{:S(2)}) copy-start(f32[128,128]{1,0:T(8,128)} %v0) | copy-start | bytes 196612
  3.6 48.2 %all-to-all-start = ((f32[8,3,128,128]{3,2,1,0:T(8,128)}), f32[8,3,128,128]{3,2,1,0:T(8,128)S(1)}, u32[]{:S(2)}, u32[]{:S(2)}) async-start(f32[8,3,128,128]{3,2,1,0:T(8,128)} %pad_maximum_fusion), calls=%async_computation | async-start | bytes 3145728 | tf_op jit(solution)/shard_map/all_to_all | solution.py:15
  11.4 12.9 %collective-permute-start.1 = (f32[128,128]{1,0:T(8,128)S(1)}, f32[128,128]{1,0:T(8,128)S(1)}, u32[]{:S(2)}, u32[]{:S(2)}) collective-permute-start(f32[128,128]{1,0:T(8,128)S(1)} %copy-done.2), channel_id=1, source_target_pairs={{0,32},{16,48},{32,0},{48,16},{1,33},{17,49},{33,1},{49,17},{2,34}... | collective-permute-start | bytes 196616 | tf_op jit(solution)/shard_map/ppermute | solution.py:19
  17.2 7.1 %collective-permute-start = (f32[128,128]{1,0:T(8,128)S(1)}, f32[128,128]{1,0:T(8,128)S(1)}, u32[]{:S(2)}, u32[]{:S(2)}) collective-permute-start(f32[128,128]{1,0:T(8,128)S(1)} %copy-done.2), channel_id=1, source_target_pairs={{0,16},{16,32},{32,48},{48,0},{1,17},{17,33},{33,49},{49,1},{2,18}... | collective-permute-start | bytes 196616 | tf_op jit(solution)/shard_map/ppermute | solution.py:19
  21.2 5.6 %collective-permute-start.2 = (f32[128,128]{1,0:T(8,128)S(1)}, f32[128,128]{1,0:T(8,128)S(1)}, u32[]{:S(2)}, u32[]{:S(2)}) collective-permute-start(f32[128,128]{1,0:T(8,128)S(1)} %copy-done.2), channel_id=1, source_target_pairs={{0,48},{16,0},{32,16},{48,32},{1,49},{17,1},{33,17},{49,33},{2,50}... | collective-permute-start | bytes 196616 | tf_op jit(solution)/shard_map/ppermute | solution.py:19
  51.8 5.4 %collective-permute-start.3 = (f32[8,3,128,128]{3,2,1,0:T(8,128)S(1)}, f32[8,3,128,128]{3,2,1,0:T(8,128)S(1)}, u32[]{:S(2)}, u32[]{:S(2)}) collective-permute-start(f32[8,3,128,128]{3,2,1,0:T(8,128)S(1)} %all-to-all-done.own), channel_id=1, source_target_pairs={{0,1},{1,0},{2,3},{3,2},{4,5},{5,4},{6,7},{7,6},{8,9},{9,8},{10,11... | collective-permute-start | bytes 4718600 | tf_op jit(solution)/shard_map/ppermute | solution.py:141
  59.9 1.3 copy-start.1
  61.2 40.8 %all-to-all-start.1 = ((f32[4,64,16,128]{3,2,1,0:T(8,128)}), f32[4,64,16,128]{3,2,1,0:T(8,128)}, u32[]{:S(2)}, u32[]{:S(2)}) async-start(f32[4,64,16,128]{3,2,1,0:T(8,128)} %copy-done.1), calls=%async_computation.1 | async-start | bytes 4194304 | tf_op jit(solution)/shard_map/all_to_all | solution.py:15
  67.2 12.0 %collective-permute-start.4 = (f32[128,128]{1,0:T(8,128)S(1)}, f32[128,128]{1,0:T(8,128)S(1)}, u32[]{:S(2)}, u32[]{:S(2)}) collective-permute-start(f32[128,128]{1,0:T(8,128)S(1)} %get-tuple-element.18), channel_id=1, source_target_pairs={{0,16},{16,32},{32,48},{48,0},{1,17},{17,33},{33,49},{49,1},{2,18}... | collective-permute-start | bytes 196616 | tf_op jit(solution)/shard_map/ppermute | solution.py:19
  71.2 9.6 %collective-permute-start.5 = (f32[128,128]{1,0:T(8,128)S(1)}, f32[128,128]{1,0:T(8,128)S(1)}, u32[]{:S(2)}, u32[]{:S(2)}) collective-permute-start(f32[128,128]{1,0:T(8,128)S(1)} %get-tuple-element.19), channel_id=1, source_target_pairs={{0,32},{16,48},{32,0},{48,16},{1,33},{17,49},{33,1},{49,17},{2,34}... | collective-permute-start | bytes 196616 | tf_op jit(solution)/shard_map/ppermute | solution.py:19
  77.0 5.4 %collective-permute-start.6 = (f32[128,128]{1,0:T(8,128)S(1)}, f32[128,128]{1,0:T(8,128)S(1)}, u32[]{:S(2)}, u32[]{:S(2)}) collective-permute-start(f32[128,128]{1,0:T(8,128)S(1)} %get-tuple-element.20), channel_id=1, source_target_pairs={{0,48},{16,0},{32,16},{48,32},{1,49},{17,1},{33,17},{49,33},{2,50}... | collective-permute-start | bytes 196616 | tf_op jit(solution)/shard_map/ppermute | solution.py:19
  82.5 4.7 %collective-permute-start.7 = (f32[4,128,128]{2,1,0:T(8,128)S(1)}, f32[4,128,128]{2,1,0:T(8,128)S(1)}, u32[]{:S(2)}, u32[]{:S(2)}) collective-permute-start(f32[4,128,128]{2,1,0:T(8,128)S(1)} %pad_maximum_fusion.2.own.z), channel_id=1, source_target_pairs={{0,1},{1,0},{2,3},{3,2},{4,5},{5,4},{6,7},{7,6},{8,9},{9,8},{10,11... | collective-permute-start | bytes 786440 | tf_op jit(solution)/shard_map/ppermute | solution.py:163
  88.3 12.7 %collective-permute-start.8 = (f32[32,8,128]{2,1,0:T(8,128)S(1)}, f32[32,8,128]{2,1,0:T(8,128)S(1)}, u32[]{:S(2)}, u32[]{:S(2)}) collective-permute-start(f32[32,8,128]{2,1,0:T(8,128)S(1)} %get-tuple-element.22), channel_id=1, source_target_pairs={{0,2},{2,4},{4,6},{6,0},{1,3},{3,5},{5,7},{7,1},{8,10},{10,12},{12... | collective-permute-start | bytes 393224 | tf_op jit(solution)/shard_map/ppermute | solution.py:19
  91.9 9.1 %collective-permute-start.9 = (f32[32,8,128]{2,1,0:T(8,128)S(1)}, f32[32,8,128]{2,1,0:T(8,128)S(1)}, u32[]{:S(2)}, u32[]{:S(2)}) collective-permute-start(f32[32,8,128]{2,1,0:T(8,128)S(1)} %get-tuple-element.23), channel_id=1, source_target_pairs={{0,4},{2,6},{4,0},{6,2},{1,5},{3,7},{5,1},{7,3},{8,12},{10,14},{12... | collective-permute-start | bytes 393224 | tf_op jit(solution)/shard_map/ppermute | solution.py:19
  96.2 5.7 %collective-permute-start.10 = (f32[32,8,128]{2,1,0:T(8,128)S(1)}, f32[32,8,128]{2,1,0:T(8,128)S(1)}, u32[]{:S(2)}, u32[]{:S(2)}) collective-permute-start(f32[32,8,128]{2,1,0:T(8,128)S(1)} %get-tuple-element.24), channel_id=1, source_target_pairs={{0,6},{2,0},{4,2},{6,4},{1,7},{3,1},{5,3},{7,5},{8,14},{10,8},{12,... | collective-permute-start | bytes 393224 | tf_op jit(solution)/shard_map/ppermute | solution.py:19
  139.8 24.4 %all-to-all-start.3 = ((f32[64,8,128]{2,1,0:T(8,128)}), f32[64,8,128]{2,1,0:T(8,128)S(1)}, u32[]{:S(2)}, u32[]{:S(2)}) async-start(f32[64,8,128]{2,1,0:T(8,128)} %broadcast_in_dim.15), calls=%async_computation.3 | async-start | bytes 524288 | tf_op jit(solution)/shard_map/all_to_all | solution.py:15

commit v5 on v4

--- a/solution.py
+++ b/solution.py
@@ -77,7 +77,7 @@
                     out[x, 16 * n + 8 * y + b] = r[at : at + 16, 128 * y : 128 * y + 128]
 
 
-def gram_two_kernel(ids, own, other, o0, o1, o2, o3, hi, lo, res):
+def gram_two_kernel(ids, own, other, after, o0, o1, o2, o3, hi, lo, res):
     for n, ref in enumerate((own, other)):
         for b in range(4):
             rows = slice(128 * n, 128 * n + 128)
@@ -161,6 +161,7 @@
     z = jnp.stack([z[0]] + [shift(z[d], "zl", NZL, d) for d in range(1, NZL)])
 
     z_other = lax.ppermute(z, "c", [(0, 1), (1, 0)])
+    core = call(core_kernel, (NY, NZL, 8, 128), 2 * 128 * 512 * 512 * 3, ids, z, *v_all)
     g2 = call(
         gram_two_kernel,
         ((32, 8, 128),) * 4,
@@ -168,10 +169,11 @@
         ids,
         z,
         z_other,
+        core,
+        unread=1,
         scratch=[pltpu.VMEM((256, 512), BF16)] * 2 + [pltpu.VMEM((512, 256), F32)],
     )
     g2 = [g2[0]] + [shift(g2[d], "x", NX, d) for d in range(1, NX)]
-    core = call(core_kernel, (NY, NZL, 8, 128), 2 * 128 * 512 * 512 * 3, ids, z, *v_all)
 
     g1 = jnp.sum(exchange(g1, "x"), axis=0)
     g2 = jnp.repeat(g2[0] + g2[1] + g2[2] + g2[3], NZH, axis=0)

time: 166 us -> 167 us (level)
    ppermute x9, waiting for transfers between devices: 6.69 us -> 9.01 us  [shift(): return lax.ppermute(a, axis, [(i, (i + d) % size) for i in range(size)])]
where the time goes in v5:
time: 167 us; the launch traced here: 166 us
  starting transfers between devices  64 us (38%)
  waiting for transfers between devices  48.1 us (29%)
  blocking collectives  36.2 us (22%)
  Pallas kernels  6.95 us (4%)
  local copies, waits for them, and re-layouts  5.69 us (3%)
  other arithmetic  4.01 us (2%)
    all_to_all x1, blocking collectives, exchange(): return lax.all_to_all(a, axes, 0, 0)  36.2 us
    all_to_all x3, waiting for transfers between devices, exchange(): return lax.all_to_all(a, axes, 0, 0)  36.2 us
    ppermute x9, starting transfers between devices, shift(): return lax.ppermute(a, axis, [(i, (i + d) % size) for i in range(size)])  35.9 us
    all_to_all x3, starting transfers between devices, exchange(): return lax.all_to_all(a, axes, 0, 0)  22.1 us
    ppermute x9, waiting for transfers between devices, shift(): return lax.ppermute(a, axis, [(i, (i + d) % size) for i in range(size)])  9.01 us
    pallas_call x4, Pallas kernels, call(): pl.pallas_call(kernel, out_shape=outs, in_specs=[pl.BlockSpec(memory_spac...  6.95 us
    unnamed x8, local copies, waits for them, and re-layouts  3.75 us
    ppermute x1, starting transfers between devices, per_device(): z_other = lax.ppermute(z, 'c', [(0, 1), (1, 0)])  3.59 us
  transfers between devices with their start and end apart: 14, of which 8 were waited for; matrix products, arithmetic and copies ran while one was open for 1% of the time, Pallas kernels for 3%

profile of v5, /device:TPU:1, one launch (start us, length us, event | category | flops | bytes accessed | tf_op | source)
XLA Modules:
  0.0 165.9 jit_solution(14729438595831060922)
XLA Ops:
  0.6 0.0 copy-start
  0.7 1.6 copy.18
  2.3 0.0 copy-done
  2.3 1.3 pad_maximum_fusion
  3.6 0.0 copy-start.2
  3.6 7.8 %all-to-all-start = ((f32[8,3,128,128]{3,2,1,0:T(8,128)}), f32[8,3,128,128]{3,2,1,0:T(8,128)S(1)}, u32[]{:S(2)}, u32[]{:S(2)}) async-start(f32[8,3,128,128]{3,2,1,0:T(8,128)} %pad_maximum_fusion), calls=%async_computation | async-start | bytes 3145728 | tf_op jit(solution)/shard_map/all_to_all | solution.py:15
  11.4 0.0 copy-done.2
  11.4 5.8 %collective-permute-start.1 = (f32[128,128]{1,0:T(8,128)S(1)}, f32[128,128]{1,0:T(8,128)S(1)}, u32[]{:S(2)}, u32[]{:S(2)}) collective-permute-start(f32[128,128]{1,0:T(8,128)S(1)} %copy-done.2), channel_id=1, source_target_pairs={{0,32},{16,48},{32,0},{48,16},{1,33},{17,49},{33,1},{49,17},{2,34}... | collective-permute-start | bytes 196616 | tf_op jit(solution)/shard_map/ppermute | solution.py:19
  17.2 4.0 %collective-permute-start = (f32[128,128]{1,0:T(8,128)S(1)}, f32[128,128]{1,0:T(8,128)S(1)}, u32[]{:S(2)}, u32[]{:S(2)}) collective-permute-start(f32[128,128]{1,0:T(8,128)S(1)} %copy-done.2), channel_id=1, source_target_pairs={{0,16},{16,32},{32,48},{48,0},{1,17},{17,33},{33,49},{49,1},{2,18}... | collective-permute-start | bytes 196616 | tf_op jit(solution)/shard_map/ppermute | solution.py:19
  21.2 3.1 %collective-permute-start.2 = (f32[128,128]{1,0:T(8,128)S(1)}, f32[128,128]{1,0:T(8,128)S(1)}, u32[]{:S(2)}, u32[]{:S(2)}) collective-permute-start(f32[128,128]{1,0:T(8,128)S(1)} %copy-done.2), channel_id=1, source_target_pairs={{0,48},{16,0},{32,16},{48,32},{1,49},{17,1},{33,17},{49,33},{2,50}... | collective-permute-start | bytes 196616 | tf_op jit(solution)/shard_map/ppermute | solution.py:19
  24.3 0.0 collective-permute-done.1.v2
  24.3 0.0 collective-permute-done.v1
  24.3 2.5 %collective-permute-done.2.v3 = f32[128,128]{1,0:T(8,128)S(1)} collective-permute-done((f32[128,128]{1,0:T(8,128)S(1)}, f32[128,128]{1,0:T(8,128)S(1)}, u32[]{:S(2)}, u32[]{:S(2)}) %collective-permute-start.2) | collective-permute-done | bytes 65568 | tf_op jit(solution)/shard_map/ppermute | solution.py:19
  26.8 25.0 %all-to-all-done.own = f32[8,3,128,128]{3,2,1,0:T(8,128)S(1)} async-done(((f32[8,3,128,128]{3,2,1,0:T(8,128)}), f32[8,3,128,128]{3,2,1,0:T(8,128)S(1)}, u32[]{:S(2)}, u32[]{:S(2)}) %all-to-all-start) | async-done | bytes 1572896 | tf_op jit(solution)/shard_map/all_to_all | solution.py:15
  51.8 2.4 %collective-permute-start.3 = (f32[8,3,128,128]{3,2,1,0:T(8,128)S(1)}, f32[8,3,128,128]{3,2,1,0:T(8,128)S(1)}, u32[]{:S(2)}, u32[]{:S(2)}) collective-permute-start(f32[8,3,128,128]{3,2,1,0:T(8,128)S(1)} %all-to-all-done.own), channel_id=1, source_target_pairs={{0,1},{1,0},{2,3},{3,2},{4,5},{5,4},{6,7},{7,6},{8,9},{9,8},{10,11... | collective-permute-start | bytes 4718600 | tf_op jit(solution)/shard_map/ppermute | solution.py:141
  54.2 0.1 pad_add_fusion.ids
  54.3 2.9 %collective-permute-done.3.other = f32[8,3,128,128]{3,2,1,0:T(8,128)S(1)} collective-permute-done((f32[8,3,128,128]{3,2,1,0:T(8,128)S(1)}, f32[8,3,128,128]{3,2,1,0:T(8,128)S(1)}, u32[]{:S(2)}, u32[]{:S(2)}) %collective-permute-start.3) | collective-permute-done | bytes 1572896 | tf_op jit(solution)/shard_map/ppermute | solution.py:141
  57.2 2.6 %shard_map.58 = f32[4,64,16,128]{3,2,1,0:T(8,128)S(1)} custom-call(s32[3]{0:T(128)S(1)} %pad_add_fusion.ids, f32[8,3,128,128]{3,2,1,0:T(8,128)S(1)} %all-to-all-done.own, f32[8,3,128,128]{3,2,1,0:T(8,128)S(1)} %collective-permute-done.3.other), custom_call_target="tpu_custom_call" | custom-call | flops 1610612736 | bytes 4194304 | tf_op jit(solution)/shard_map/pallas_call | solution.py:118
  59.9 0.0 copy-start.1
  59.9 1.3 copy-done.1
  61.2 4.4 %all-to-all-start.1 = ((f32[4,64,16,128]{3,2,1,0:T(8,128)}), f32[4,64,16,128]{3,2,1,0:T(8,128)}, u32[]{:S(2)}, u32[]{:S(2)}) async-start(f32[4,64,16,128]{3,2,1,0:T(8,128)} %copy-done.1), calls=%async_computation.1 | async-start | bytes 4194304 | tf_op jit(solution)/shard_map/all_to_all | solution.py:15
  65.6 1.6 shard_map.59
  67.2 4.0 %collective-permute-start.4 = (f32[128,128]{1,0:T(8,128)S(1)}, f32[128,128]{1,0:T(8,128)S(1)}, u32[]{:S(2)}, u32[]{:S(2)}) collective-permute-start(f32[128,128]{1,0:T(8,128)S(1)} %get-tuple-element.18), channel_id=1, source_target_pairs={{0,16},{16,32},{32,48},{48,0},{1,17},{17,33},{33,49},{49,1},{2,18}... | collective-permute-start | bytes 196616 | tf_op jit(solution)/shard_map/ppermute | solution.py:19
  71.2 5.8 %collective-permute-start.5 = (f32[128,128]{1,0:T(8,128)S(1)}, f32[128,128]{1,0:T(8,128)S(1)}, u32[]{:S(2)}, u32[]{:S(2)}) collective-permute-start(f32[128,128]{1,0:T(8,128)S(1)} %get-tuple-element.19), channel_id=1, source_target_pairs={{0,32},{16,48},{32,0},{48,16},{1,33},{17,49},{33,1},{49,17},{2,34}... | collective-permute-start | bytes 196616 | tf_op jit(solution)/shard_map/ppermute | solution.py:19
  77.0 2.2 %collective-permute-start.6 = (f32[128,128]{1,0:T(8,128)S(1)}, f32[128,128]{1,0:T(8,128)S(1)}, u32[]{:S(2)}, u32[]{:S(2)}) collective-permute-start(f32[128,128]{1,0:T(8,128)S(1)} %get-tuple-element.20), channel_id=1, source_target_pairs={{0,48},{16,0},{32,16},{48,32},{1,49},{17,1},{33,17},{49,33},{2,50}... | collective-permute-start | bytes 196616 | tf_op jit(solution)/shard_map/ppermute | solution.py:19
  79.2 0.0 collective-permute-done.4
  79.2 1.6 collective-permute-done.5
  80.9 1.6 collective-permute-done.6
  82.5 3.6 %collective-permute-start.7 = (f32[4,128,128]{2,1,0:T(8,128)S(1)}, f32[4,128,128]{2,1,0:T(8,128)S(1)}, u32[]{:S(2)}, u32[]{:S(2)}) collective-permute-start(f32[4,128,128]{2,1,0:T(8,128)S(1)} %pad_maximum_fusion.2.z.own), channel_id=1, source_target_pairs={{0,1},{1,0},{2,3},{3,2},{4,5},{5,4},{6,7},{7,6},{8,9},{9,8},{10,11... | collective-permute-start | bytes 786440 | tf_op jit(solution)/shard_map/ppermute | solution.py:163
  86.1 1.6 shard_map.60.after
  87.7 0.0 collective-permute-done.7.other
  87.7 1.1 shard_map.61
  88.8 3.6 %collective-permute-start.8 = (f32[32,8,128]{2,1,0:T(8,128)S(1)}, f32[32,8,128]{2,1,0:T(8,128)S(1)}, u32[]{:S(2)}, u32[]{:S(2)}) collective-permute-start(f32[32,8,128]{2,1,0:T(8,128)S(1)} %get-tuple-element.26), channel_id=1, source_target_pairs={{0,2},{2,4},{4,6},{6,0},{1,3},{3,5},{5,7},{7,1},{8,10},{10,12},{12... | collective-permute-start | bytes 393224 | tf_op jit(solution)/shard_map/ppermute | solution.py:19
  92.4 4.3 %collective-permute-start.9 = (f32[32,8,128]{2,1,0:T(8,128)S(1)}, f32[32,8,128]{2,1,0:T(8,128)S(1)}, u32[]{:S(2)}, u32[]{:S(2)}) collective-permute-start(f32[32,8,128]{2,1,0:T(8,128)S(1)} %get-tuple-element.27), channel_id=1, source_target_pairs={{0,4},{2,6},{4,0},{6,2},{1,5},{3,7},{5,1},{7,3},{8,12},{10,14},{12... | collective-permute-start | bytes 393224 | tf_op jit(solution)/shard_map/ppermute | solution.py:19
  96.8 3.1 %collective-permute-start.10 = (f32[32,8,128]{2,1,0:T(8,128)S(1)}, f32[32,8,128]{2,1,0:T(8,128)S(1)}, u32[]{:S(2)}, u32[]{:S(2)}) collective-permute-start(f32[32,8,128]{2,1,0:T(8,128)S(1)} %get-tuple-element.28), channel_id=1, source_target_pairs={{0,6},{2,0},{4,2},{6,4},{1,7},{3,1},{5,3},{7,5},{8,14},{10,8},{12,... | collective-permute-start | bytes 393224 | tf_op jit(solution)/shard_map/ppermute | solution.py:19
  99.9 0.0 collective-permute-done.8
  99.9 1.4 collective-permute-done.9
  101.3 1.8 %collective-permute-done.10 = f32[32,8,128]{2,1,0:T(8,128)S(1)} collective-permute-done((f32[32,8,128]{2,1,0:T(8,128)S(1)}, f32[32,8,128]{2,1,0:T(8,128)S(1)}, u32[]{:S(2)}, u32[]{:S(2)}) %collective-permute-start.10) | collective-permute-done | bytes 131104 | tf_op jit(solution)/shard_map/ppermute | solution.py:19
  103.2 0.0 all-to-all-done.1
  103.2 1.8 %reduce_sum.27 = f32[64,16,128]{2,1,0:T(8,128)S(1)} reduce(f32[4,64,16,128]{3,2,1,0:T(8,128)} %all-to-all-done.1, f32[]{:T(128)} %constant.30.clone.1), dimensions={0}, to_apply=%region_0.0 | reduce | flops 393216 | bytes 2621444 | tf_op jit(solution)/shard_map/reduce_sum | solution.py:178
  105.0 0.1 pad_maximum_fusion.1
  105.1 36.2 %all_to_all.20 = f32[64,32,128]{2,1,0:T(8,128)S(1)} all-to-all(f32[64,32,128]{2,1,0:T(8,128)S(1)} %pad_maximum_fusion.1), channel_id=1, replica_groups=mesh['yh'=2,'yl'=4,'zl'=4,'zh'=2,'x'=4,'c'=2] {'yh','yl','zl','zh'}, dimensions={0} | all-to-all | bytes 2097152 | tf_op jit(solution)/shard_map/all_to_all | solution.py:15
  141.3 0.1 slice_reduce_fusion.1
  141.4 0.7 broadcast_in_dim.15
  142.1 9.9 %all-to-all-start.3 = ((f32[64,8,128]{2,1,0:T(8,128)}), f32[64,8,128]{2,1,0:T(8,128)S(1)}, u32[]{:S(2)}, u32[]{:S(2)}) async-start(f32[64,8,128]{2,1,0:T(8,128)} %broadcast_in_dim.15), calls=%async_computation.3 | async-start | bytes 524288 | tf_op jit(solution)/shard_map/all_to_all | solution.py:15
  152.1 0.2 reshape.34
  152.4 0.1 copy.15
  152.5 0.8 copy.16
  153.3 0.1 slice_reduce_fusion
  153.4 0.6 multiply_bitcast_fusion
  154.0 11.2 %all-to-all-done.3 = f32[64,8,128]{2,1,0:T(8,128)S(1)} async-done(((f32[64,8,128]{2,1,0:T(8,128)}), f32[64,8,128]{2,1,0:T(8,128)S(1)}, u32[]{:S(2)}, u32[]{:S(2)}) %all-to-all-start.3) | async-done | bytes 262176 | tf_op jit(solution)/shard_map/all_to_all | solution.py:15
  165.2 0.7 copy.13
  (10 shorter events, 0.2 us)
Async XLA Ops:
  0.6 1.6 copy-start
  3.6 7.8 %copy-start.2 = (f32[128,128]{1,0:T(8,128)S(1)}, f32[128,128]{1,0:T(8,128)}, u32[]{:S(2)}) copy-start(f32[128,128]{1,0:T(8,128)} %v0) | copy-start | bytes 196612
  3.6 48.2 %all-to-all-start = ((f32[8,3,128,128]{3,2,1,0:T(8,128)}), f32[8,3,128,128]{3,2,1,0:T(8,128)S(1)}, u32[]{:S(2)}, u32[]{:S(2)}) async-start(f32[8,3,128,128]{3,2,1,0:T(8,128)} %pad_maximum_fusion), calls=%async_computation | async-start | bytes 3145728 | tf_op jit(solution)/shard_map/all_to_all | solution.py:15
  11.4 12.9 %collective-permute-start.1 = (f32[128,128]{1,0:T(8,128)S(1)}, f32[128,128]{1,0:T(8,128)S(1)}, u32[]{:S(2)}, u32[]{:S(2)}) collective-permute-start(f32[128,128]{1,0:T(8,128)S(1)} %copy-done.2), channel_id=1, source_target_pairs={{0,32},{16,48},{32,0},{48,16},{1,33},{17,49},{33,1},{49,17},{2,34}... | collective-permute-start | bytes 196616 | tf_op jit(solution)/shard_map/ppermute | solution.py:19
  17.2 7.1 %collective-permute-start = (f32[128,128]{1,0:T(8,128)S(1)}, f32[128,128]{1,0:T(8,128)S(1)}, u32[]{:S(2)}, u32[]{:S(2)}) collective-permute-start(f32[128,128]{1,0:T(8,128)S(1)} %copy-done.2), channel_id=1, source_target_pairs={{0,16},{16,32},{32,48},{48,0},{1,17},{17,33},{33,49},{49,1},{2,18}... | collective-permute-start | bytes 196616 | tf_op jit(solution)/shard_map/ppermute | solution.py:19
  21.2 5.6 %collective-permute-start.2 = (f32[128,128]{1,0:T(8,128)S(1)}, f32[128,128]{1,0:T(8,128)S(1)}, u32[]{:S(2)}, u32[]{:S(2)}) collective-permute-start(f32[128,128]{1,0:T(8,128)S(1)} %copy-done.2), channel_id=1, source_target_pairs={{0,48},{16,0},{32,16},{48,32},{1,49},{17,1},{33,17},{49,33},{2,50}... | collective-permute-start | bytes 196616 | tf_op jit(solution)/shard_map/ppermute | solution.py:19
  51.8 5.4 %collective-permute-start.3 = (f32[8,3,128,128]{3,2,1,0:T(8,128)S(1)}, f32[8,3,128,128]{3,2,1,0:T(8,128)S(1)}, u32[]{:S(2)}, u32[]{:S(2)}) collective-permute-start(f32[8,3,128,128]{3,2,1,0:T(8,128)S(1)} %all-to-all-done.own), channel_id=1, source_target_pairs={{0,1},{1,0},{2,3},{3,2},{4,5},{5,4},{6,7},{7,6},{8,9},{9,8},{10,11... | collective-permute-start | bytes 4718600 | tf_op jit(solution)/shard_map/ppermute | solution.py:141
  59.9 1.3 copy-start.1
  61.2 42.0 %all-to-all-start.1 = ((f32[4,64,16,128]{3,2,1,0:T(8,128)}), f32[4,64,16,128]{3,2,1,0:T(8,128)}, u32[]{:S(2)}, u32[]{:S(2)}) async-start(f32[4,64,16,128]{3,2,1,0:T(8,128)} %copy-done.1), calls=%async_computation.1 | async-start | bytes 4194304 | tf_op jit(solution)/shard_map/all_to_all | solution.py:15
  67.2 12.0 %collective-permute-start.4 = (f32[128,128]{1,0:T(8,128)S(1)}, f32[128,128]{1,0:T(8,128)S(1)}, u32[]{:S(2)}, u32[]{:S(2)}) collective-permute-start(f32[128,128]{1,0:T(8,128)S(1)} %get-tuple-element.18), channel_id=1, source_target_pairs={{0,16},{16,32},{32,48},{48,0},{1,17},{17,33},{33,49},{49,1},{2,18}... | collective-permute-start | bytes 196616 | tf_op jit(solution)/shard_map/ppermute | solution.py:19
  71.2 9.6 %collective-permute-start.5 = (f32[128,128]{1,0:T(8,128)S(1)}, f32[128,128]{1,0:T(8,128)S(1)}, u32[]{:S(2)}, u32[]{:S(2)}) collective-permute-start(f32[128,128]{1,0:T(8,128)S(1)} %get-tuple-element.19), channel_id=1, source_target_pairs={{0,32},{16,48},{32,0},{48,16},{1,33},{17,49},{33,1},{49,17},{2,34}... | collective-permute-start | bytes 196616 | tf_op jit(solution)/shard_map/ppermute | solution.py:19
  77.0 5.4 %collective-permute-start.6 = (f32[128,128]{1,0:T(8,128)S(1)}, f32[128,128]{1,0:T(8,128)S(1)}, u32[]{:S(2)}, u32[]{:S(2)}) collective-permute-start(f32[128,128]{1,0:T(8,128)S(1)} %get-tuple-element.20), channel_id=1, source_target_pairs={{0,48},{16,0},{32,16},{48,32},{1,49},{17,1},{33,17},{49,33},{2,50}... | collective-permute-start | bytes 196616 | tf_op jit(solution)/shard_map/ppermute | solution.py:19
  82.5 5.3 %collective-permute-start.7 = (f32[4,128,128]{2,1,0:T(8,128)S(1)}, f32[4,128,128]{2,1,0:T(8,128)S(1)}, u32[]{:S(2)}, u32[]{:S(2)}) collective-permute-start(f32[4,128,128]{2,1,0:T(8,128)S(1)} %pad_maximum_fusion.2.z.own), channel_id=1, source_target_pairs={{0,1},{1,0},{2,3},{3,2},{4,5},{5,4},{6,7},{7,6},{8,9},{9,8},{10,11... | collective-permute-start | bytes 786440 | tf_op jit(solution)/shard_map/ppermute | solution.py:163
  88.8 11.0 %collective-permute-start.8 = (f32[32,8,128]{2,1,0:T(8,128)S(1)}, f32[32,8,128]{2,1,0:T(8,128)S(1)}, u32[]{:S(2)}, u32[]{:S(2)}) collective-permute-start(f32[32,8,128]{2,1,0:T(8,128)S(1)} %get-tuple-element.26), channel_id=1, source_target_pairs={{0,2},{2,4},{4,6},{6,0},{1,3},{3,5},{5,7},{7,1},{8,10},{10,12},{12... | collective-permute-start | bytes 393224 | tf_op jit(solution)/shard_map/ppermute | solution.py:19
  92.4 8.8 %collective-permute-start.9 = (f32[32,8,128]{2,1,0:T(8,128)S(1)}, f32[32,8,128]{2,1,0:T(8,128)S(1)}, u32[]{:S(2)}, u32[]{:S(2)}) collective-permute-start(f32[32,8,128]{2,1,0:T(8,128)S(1)} %get-tuple-element.27), channel_id=1, source_target_pairs={{0,4},{2,6},{4,0},{6,2},{1,5},{3,7},{5,1},{7,3},{8,12},{10,14},{12... | collective-permute-start | bytes 393224 | tf_op jit(solution)/shard_map/ppermute | solution.py:19
  96.8 6.4 %collective-permute-start.10 = (f32[32,8,128]{2,1,0:T(8,128)S(1)}, f32[32,8,128]{2,1,0:T(8,128)S(1)}, u32[]{:S(2)}, u32[]{:S(2)}) collective-permute-start(f32[32,8,128]{2,1,0:T(8,128)S(1)} %get-tuple-element.28), channel_id=1, source_target_pairs={{0,6},{2,0},{4,2},{6,4},{1,7},{3,1},{5,3},{7,5},{8,14},{10,8},{12,... | collective-permute-start | bytes 393224 | tf_op jit(solution)/shard_map/ppermute | solution.py:19
  142.1 23.1 %all-to-all-start.3 = ((f32[64,8,128]{2,1,0:T(8,128)}), f32[64,8,128]{2,1,0:T(8,128)S(1)}, u32[]{:S(2)}, u32[]{:S(2)}) async-start(f32[64,8,128]{2,1,0:T(8,128)} %broadcast_in_dim.15), calls=%async_computation.3 | async-start | bytes 524288 | tf_op jit(solution)/shard_map/all_to_all | solution.py:15
